TPU v7x, 128 devices: a whole 4x4x4 slice. The times are simulated.
128 devices in a mesh: dp: 16 (over z_hi, y, core), tensor: 8 (over z_lo, x).
Axes of the slice: x: 4, y: 4, z: 4 (z_hi: 2, z_lo: 2; z = z_hi * 2 + z_lo), core: 2. Of those that a mesh axis runs over, the one named last changes fastest.
Arguments:
- train_inputs: bfloat16 [32, 512, 4096], P('dp', None, 'tensor'), may hold values from -100 to 100
- train_grads: bfloat16 [32, 2, 512, 14336], P('dp', None, None, 'tensor'), may hold values from -100 to 100
- train_lengths: int32 [32], P('dp'), may hold values from 64 to 512, as said below
- query_inputs: bfloat16 [256, 128, 4096], P('dp', None, 'tensor'), may hold values from -100 to 100
- query_grads: bfloat16 [256, 2, 128, 14336], P('dp', None, None, 'tensor'), may hold values from -100 to 100
- query_lengths: int32 [256], P('dp'), may hold values from 16 to 128, as said below
- proj_in: bfloat16 [4096, 64], P('tensor'), may hold values from -0.09375 to 0.09375
- proj_out: bfloat16 [2, 14336, 64], P(None, 'tensor'), may hold values from -0.046875 to 0.046875
Outputs:
- scores: float32 [32, 256], P('dp')
Inputs may be any that keep to these rules, and one draw needn't show every extreme that they name: `train_lengths`: some training sequence has exactly 512 live positions. `query_lengths`: some query generation has exactly 128 live positions.
All inputs are finite; a program needn't handle non-finite values.
Results may differ from a plain program's by a relative error of at most 0.0061.
Values sent between devices are 32-bit elements; how exact they have to be, the bound alone decides.
A program may use at most 128 MiB of HBM per device.

v0:
```python
import math

import jax
import jax.numpy as jnp
from jax import lax
from jax.sharding import PartitionSpec as P

damping = 0.1


def damped(moment):
    size_r = moment.shape[-1]
    return moment + damping * jnp.trace(moment) / size_r * jnp.eye(size_r, dtype=jnp.float32)


def condition_one(sketch, chol_out, chol_in):
    left_solve = jax.scipy.linalg.cho_solve((chol_out, True), sketch)
    return jax.scipy.linalg.cho_solve((chol_in, True), left_solve.T).T


def local_vectors(inputs, gradient, proj_in, proj_out):
    input_part = jnp.einsum("esd,dr->esr", inputs, proj_in, preferred_element_type=jnp.float32)
    output_part = jnp.einsum(
        "eksf,kfr->eskr", gradient, proj_out, preferred_element_type=jnp.float32
    )
    dims_out = output_part.shape
    return (input_part, output_part.reshape(dims_out[0], dims_out[1], dims_out[2] * dims_out[3]))


def finish_vectors(input_part, output_part, lengths):
    seq_len = input_part.shape[1]
    position = lax.broadcasted_iota(jnp.int32, (1, seq_len), 1)
    keeper = (position < lengths[:, None]).astype(jnp.float32)[:, :, None]
    input_proj = (input_part * keeper).astype(jnp.bfloat16)
    output_proj = (output_part * keeper).astype(jnp.bfloat16)
    sketch = jnp.einsum("esk,esr->ekr", output_proj, input_proj, preferred_element_type=jnp.float32)
    return (input_proj, output_proj, sketch, jnp.sum(keeper))


def second_moments(input_proj, output_proj, ranks):
    in_moment = jnp.einsum(
        "esr,esq->rq", input_proj, input_proj, preferred_element_type=jnp.float32
    )
    dims_out = output_proj.shape
    grouped = output_proj.reshape(dims_out[0], dims_out[1], dims_out[2] // ranks, ranks)
    out_moment = jnp.einsum("eskr,eskq->krq", grouped, grouped, preferred_element_type=jnp.float32)
    return (in_moment, out_moment)


def on_device(
    train_inputs,
    train_grads,
    train_lengths,
    query_inputs,
    query_grads,
    query_lengths,
    proj_in,
    proj_out,
):
    ranks = proj_in.shape[1]
    train_seq = train_inputs.shape[1]
    query_seq = query_inputs.shape[1]
    score_scale = 1.0 / (ranks * math.sqrt(train_seq * query_seq))
    train_in, train_out = local_vectors(train_inputs, train_grads, proj_in, proj_out)
    query_in, query_out = local_vectors(query_inputs, query_grads, proj_in, proj_out)
    train_in, train_out, query_in, query_out = lax.psum(
        (train_in, train_out, query_in, query_out), "tensor"
    )
    train_in, train_out, train_sketch, train_live = finish_vectors(
        train_in, train_out, train_lengths
    )
    query_sketch = finish_vectors(query_in, query_out, query_lengths)[2]
    in_moment, out_moment = second_moments(train_in, train_out, ranks)
    in_moment, out_moment, total_live = lax.psum((in_moment, out_moment, train_live), "dp")
    chol_in = jnp.linalg.cholesky(damped(in_moment / total_live))
    chol_out = jax.vmap(lambda moment: jnp.linalg.cholesky(damped(moment)))(out_moment / total_live)
    train_count = train_sketch.shape[0]
    layers_n = chol_out.shape[0]
    conditioned = jax.vmap(jax.vmap(condition_one, in_axes=(0, 0, None)), in_axes=(0, None, None))(
        train_sketch.reshape(train_count, layers_n, ranks, ranks), chol_out, chol_in
    ).reshape(train_count, -1)
    query_flat = query_sketch.reshape(query_sketch.shape[0], -1)
    return (
        lax.dot_general(
            conditioned,
            lax.all_gather(query_flat, "dp", axis=0, tiled=True),
            (((1,), (1,)), ((), ())),
            precision=lax.Precision.HIGHEST,
            preferred_element_type=jnp.float32,
        )
        * score_scale
    )


def solution(mesh):
    placed = (
        P("dp", None, "tensor"),
        P("dp", None, None, "tensor"),
        P("dp"),
        P("dp", None, "tensor"),
        P("dp", None, None, "tensor"),
        P("dp"),
        P("tensor", None),
        P(None, "tensor", None),
    )
    return jax.shard_map(
        on_device, mesh=mesh, in_specs=placed, out_specs=P("dp", None), check_vma=False
    )
```

profile of v0, /device:TPU:0, one launch (start us, length us, event | category | flops | bytes accessed | tf_op | source)
XLA Modules:
  0.0 244.6 jit_solution(9976510039568018857)
XLA Ops:
  6.6 5.7 %fusion.7 = f32[2,512,2,64]{1,3,0,2:T(8,128)S(1)} fusion(bf16[2,2,512,1792]{3,2,1,0:T(8,128)(2,1)} %param.9, bf16[2,1792,64]{1,2,0:T(8,128)(2,1)} %param.15), kind=kOutput, calls=%fused_computation.5 | convolution fusion | flops 469762048 | bytes 8323072 | tf_op jit(solution)/shard_map/eksf,kfr->eskr/dot_general | solution.py:23
  12.2 0.9 copy.34
  13.1 1.2 fusion.24
  14.3 1.5 fusion.22
  15.8 7.7 %fusion.4 = f32[16,128,2,64]{1,3,0,2:T(8,128)S(1)} fusion(bf16[16,2,128,1792]{3,2,1,0:T(8,128)(2,1)} %param.12, bf16[2,1792,64]{1,2,0:T(8,128)(2,1)S(1)} %copy-done.5), kind=kOutput, calls=%fused_computation.4 | convolution fusion | flops 939524096 | bytes 16187392 | tf_op jit(solution)/shard_map/eksf,kfr->eskr/dot_general | solution.py:23
  23.6 1.2 copy.48
  24.7 0.0 all-reduce.4.cloned.1.call-update
  24.8 0.0 all-gather.2.cloned.1.call-start
  24.8 0.1 fusion.32
  24.9 86.8 %all-reduce.4.cloned.1.call-done = (f32[2,512,128]{1,2,0:T(8,128)}, f32[2,512,64]{1,2,0:T(8,128)}, f32[16,128,128]{1,2,0:T(8,128)}, f32[16,128,64]{1,2,0:T(8,128)}) async-done(((f32[2,512,128]{1,2,0:T(8,128)}, f32[2,512,64]{1,2,0:T(8,128)}, f32[16,128,128]{1,2,0:T(8,128)}, f32[16,128,64]{1,2,0:T(8,128)}), (f32[2,512,128]{1,2,0:T(8,128)}, f32[2,512,64]{1,2,0:T(8,128)}, f32[16,128,128]{1,2,0:T(8,128)}, ...) | async-done | bytes 2359312 | tf_op jit(solution)/shard_map/psum | solution.py:66
  111.7 1.6 fusion.10
  113.3 1.2 reshape.151
  114.5 0.0 all-gather.2.cloned.1.call-update
  114.6 0.7 fusion.33
  115.3 0.1 compare_convert_fusion.1
  115.4 1.1 multiply_convert_fusion.3
  116.5 1.2 fusion.26
  117.6 0.1 reshape.143
  117.7 0.1 copy.37
  117.9 1.2 convolution_bitcast_fusion.2
  119.1 0.2 convolution_bitcast_fusion.1
  119.3 67.9 %all-reduce = (f32[2,64,64]{2,1,0:T(8,128)S(1)}, f32[]{:T(128)}, f32[64,64]{1,0:T(8,128)S(1)}) all-reduce(f32[2,64,64]{2,1,0:T(8,128)S(1)} %convolution_bitcast_fusion.1, f32[]{:T(128)} %fusion.33, f32[64,64]{1,0:T(8,128)S(1)} %convolution_bitcast_fusion.2), channel_id=1, replica_groups=mesh['dp'=16,'tensor'=8] {'dp'}, use_global_device_ids=true, to_apply=%region_8.9 | all-reduce | flops 12289 | bytes 98312 | tf_op jit(solution)/shard_map/psum | solution.py:74
  187.1 1.2 select_reduce_fusion.3
  188.9 0.7 select_add_fusion
  189.6 0.1 copy.32
  189.7 0.7 fusion.30
  190.4 5.8 %cholesky.32 = f32[64,64]{1,0:T(8,128)S(1)} custom-call(f32[64,64]{1,0:T(8,128)S(1)} %fusion.30), custom_call_target="Cholesky" | custom-call | tf_op jit(solution)/shard_map/jit(cholesky)/cholesky | solution.py:75
  196.2 0.6 compare_reduce_fusion.1
  196.9 0.6 fusion.27
  197.4 4.9 %custom-call.21 = f32[1,64,64]{1,2,0:T(8,128)S(1)} custom-call(f32[1,64,64]{2,1,0:T(8,128)S(1)} %fusion.27), custom_call_target="InvertDiagBlocksLowerTriangular" | custom-call | tf_op jit(solution)/shard_map/vmap(vmap(jit(_cho_solve)))/triangular_solve | solution.py:18
  202.3 0.8 select_reduce_fusion.1
  203.1 0.7 multiply_add_fusion
  203.8 0.1 copy.35
  203.9 0.7 fusion.21
  204.7 11.7 %custom-call.22 = f32[2,64,64]{2,1,0:T(8,128)S(1)} custom-call(f32[2,64,64]{2,1,0:T(8,128)S(1)} %fusion.21), custom_call_target="Cholesky" | custom-call | tf_op jit(solution)/shard_map/vmap(jit(cholesky))/cholesky | solution.py:76
  216.4 0.1 compare_reduce_fusion
  216.5 0.1 select_bitcast_fusion
  216.6 9.8 %custom-call.23 = f32[2,1,64,64]{2,3,1,0:T(8,128)S(1)} custom-call(f32[2,1,64,64]{3,2,1,0:T(8,128)S(1)} %select_bitcast_fusion), custom_call_target="InvertDiagBlocksLowerTriangular" | custom-call | tf_op jit(solution)/shard_map/vmap(vmap(jit(_cho_solve)))/triangular_solve | solution.py:17
  226.5 0.4 fusion.19
  226.9 0.4 fusion.17
  227.3 0.1 copy.41
  227.4 0.1 copy.71
  227.5 0.3 fusion.15
  227.8 0.2 convolution_bitcast_fusion
  228.0 0.1 copy.45
  228.1 0.1 reshape.149
  228.3 0.0 all-gather.2.cloned.1.call-done
  228.3 9.5 %convolution_multiply_fusion = f32[2,256]{1,0:T(2,128)} fusion(f32[2,8192]{1,0:T(2,128)S(1)} %reshape.149, f32[256,8192]{1,0:T(8,128)} %all-gather.2.cloned.1.call-done), kind=kOutput, calls=%fused_computation.9 | convolution fusion | flops 50332160 | bytes 8456192 | tf_op jit(solution)/shard_map/dot_general | solution.py:84
  (20 shorter events, 0.1 us)
Async XLA Ops:
  6.5 7.7 %copy-start = (bf16[16,128,512]{2,1,0:T(8,128)(2,1)S(1)}, bf16[16,128,512]{2,1,0:T(8,128)(2,1)}, u32[]{:S(2)}) copy-start(bf16[16,128,512]{2,1,0:T(8,128)(2,1)} %param.11) | copy-start | bytes 6291460
  6.5 6.6 %copy-start.2 = (bf16[512,64]{0,1:T(8,128)(2,1)S(1)}, bf16[512,64]{0,1:T(8,128)(2,1)}, u32[]{:S(2)}) copy-start(bf16[512,64]{0,1:T(8,128)(2,1)} %param.14) | copy-start | bytes 196612
  6.5 6.6 %copy-start.1 = (bf16[2,512,512]{2,1,0:T(8,128)(2,1)S(1)}, bf16[2,512,512]{2,1,0:T(8,128)(2,1)}, u32[]{:S(2)}) copy-start(bf16[2,512,512]{2,1,0:T(8,128)(2,1)} %param.8) | copy-start | bytes 3145732
  6.5 105.1 %all-reduce.4.cloned.1.call-start = ((), (), s32[]{:S(2)}) async-start(), calls=%async_computation.1 | async-start | bytes 4718592 | tf_op jit(solution)/shard_map/psum | solution.py:66
  6.5 9.3 %copy-start.5 = (bf16[2,1792,64]{1,2,0:T(8,128)(2,1)S(1)}, bf16[2,1792,64]{1,2,0:T(8,128)(2,1)}, u32[]{:S(2)}) copy-start(bf16[2,1792,64]{1,2,0:T(8,128)(2,1)} %param.15) | copy-start | bytes 1376260
  15.8 9.0 %copy-start.3 = (s32[16]{0:T(128)S(1)}, s32[16]{0:T(128)}, u32[]{:S(2)}) copy-start(s32[16]{0:T(128)} %param.13) | copy-start | bytes 196
  23.6 91.0 %copy-start.4 = (s32[2]{0:T(128)S(1)}, s32[2]{0:T(128)}, u32[]{:S(2)}) copy-start(s32[2]{0:T(128)} %param.10) | copy-start | bytes 28
  24.8 203.5 %all-gather.2.cloned.1.call-start = ((), (), s32[]{:S(2)}) async-start(), calls=%async_computation | async-start | bytes 8912896 | tf_op jit(solution)/shard_map/all_gather | solution.py:86
Sparse Core Ops, SparseCore 0:
  24.9 86.7 all-reduce.3
  114.7 73.5 all-gather.1
where the time goes:
time: 245 us
  waiting for transfers between devices  86.8 us (35%)
  blocking collectives  67.9 us (28%)
  other arithmetic  40.5 us (17%)
  matrix products  31.1 us (13%)
  between operations  14.2 us (6%)
  local copies, waits for them, and re-layouts  4.1 us (2%)
    psum x1, waiting for transfers between devices, on_device(): lax.psum((train_in, train_out, query_in, query_out), 'tensor')  86.8 us
    psum x1, blocking collectives, on_device(): lax.psum((in_moment, out_moment, train_live), 'dp')  67.9 us
    dot_general x2, matrix products, local_vectors(): jnp.einsum('eksf,kfr->eskr', gradient, proj_out, preferred_element_type=j...  13.4 us
    another operation x3, other arithmetic, on_device(): jnp.linalg.cholesky(damped(moment))  11.9 us
    another operation x2, other arithmetic, condition_one(): left_solve = jax.scipy.linalg.cho_solve((chol_out, True), sketch)  9.91 us
    dot_general x1, matrix products, on_device(): lax.dot_general(conditioned, lax.all_gather(query_flat, 'dp', axis=0, til...  9.49 us
    another operation x4, other arithmetic, on_device(): chol_in = jnp.linalg.cholesky(damped(in_moment / total_live))  6.5 us
    another operation x3, other arithmetic, condition_one(): return jax.scipy.linalg.cho_solve((chol_in, True), left_solve.T).T  5.48 us
  transfers between devices with their start and end apart: 2, of which 1 were waited for; matrix products, arithmetic and copies ran while one was open for 18% of the time, Pallas kernels for 0%

commit v1 on v0

v1 whole, which is shorter than its diff:
```python
import functools
import math

import jax
import jax.numpy as jnp
from jax import lax
from jax.experimental import pallas as pl
from jax.experimental.pallas import tpu as pltpu
from jax.sharding import PartitionSpec as P

MESH = pl.DeviceIdType.MESH
F32 = jnp.float32
BF16 = jnp.bfloat16
DAMPING = 0.1
RANK = 64
BLOCK = 128
HALF = 64
TENSOR = 8
DP = 16
GENS = ((1, 3, 4), (3, 4, 1), (4, 1, 3))
DOUBLINGS = 7


def chebyshev():
    low = DAMPING / RANK
    high = 1.0 + low
    angle = math.acosh((high + low) / (high - low))
    gains = []
    n = 1
    for _ in range(DOUBLINGS):
        gains.append(2.0 * math.cosh(n * angle) ** 2 / math.cosh(2 * n * angle))
        n *= 2
    return 2.0 / (high + low), gains


def rem(a, b):
    return lax.rem(a, jnp.int32(b))


def div(a, b):
    return lax.div(a, jnp.int32(b))


def split(v):
    high = v.astype(BF16)
    return high, (v - high.astype(F32)).astype(BF16)


def kernel(
    tlen, qlen, tin, tgr, qin, qgr, pin, pout, out_ref,
    xin, xgr, win, wout, wip, wop,
    acc, recv1, recv2, recv3,
    mloc, mrecv1, msum, mrecv2, mfull,
    bloc, brecv1, bsum, ball,
    qall, msg, fin,
    lsem, wsem, s1, r1, s2, r2, s3, r3,
    ms1, mr1, ms2, mr2, ms3, mr3,
    bs1, br1, bs2, br2, qs, qr, fs, fr,
):
    d = lax.axis_index("dp").astype(jnp.int32)
    t = lax.axis_index("tensor").astype(jnp.int32)
    z, x = div(t, 4), rem(t, 4)

    def flip(m):
        m = jnp.int32(m)
        mx, mz = rem(m, 4), div(m, 4)
        low = rem(x + mx, 2)
        high = rem(div(x, 2) + div(mx, 2), 2)
        return rem(z + mz, 2) * 4 + high * 2 + low

    def remote(src, dst, ssem, rsem, dd, tt):
        return pltpu.make_async_remote_copy(
            src_ref=src, dst_ref=dst, send_sem=ssem, recv_sem=rsem,
            device_id=(dd, tt), device_id_type=MESH,
        )

    def load(r, j):
        item = flip(7 - j)
        slot = r * 8 + j
        if r == 0:
            e, p = div(item, 4), rem(item, 4)
            rows = pl.ds(pl.multiple_of(p * BLOCK, BLOCK), BLOCK)
            a, b = tin.at[e, rows, :], tgr.at[e, :, rows, :]
        else:
            q = item * 2 + (r - 1)
            a, b = qin.at[q], qgr.at[q]
        return (
            pltpu.make_async_copy(a, xin.at[slot], lsem.at[0, slot]),
            pltpu.make_async_copy(b, xgr.at[slot], lsem.at[1, slot]),
        )

    def start_load(r, j):
        for c in load(r, j):
            c.start()

    wcopies = (
        pltpu.make_async_copy(pin, win, wsem.at[0]),
        pltpu.make_async_copy(pout, wout, wsem.at[1]),
    )
    for c in wcopies:
        c.start()

    @pl.loop(0, 8)
    def _(j):
        start_load(0, j)

    barrier = pltpu.get_barrier_semaphore()

    def greet(dd, tt):
        pl.semaphore_signal(barrier, inc=1, device_id=(dd, tt), device_id_type=MESH)

    def is_me(dd, tt):
        return jnp.logical_and(dd == d, tt == t)

    @pl.loop(1, 8)
    def _(m):
        greet(d, flip(m))

    @pl.loop(1, 16)
    def _(j):
        greet(rem(d + j, DP), t)

    @pl.loop(0, 16)
    def _(j):
        dd, tt = t * 2 + div(j, 8), rem(j, 8)

        @pl.when(jnp.logical_not(is_me(dd, tt)))
        def _():
            greet(dd, tt)

        column = div(d, 2)

        @pl.when(jnp.logical_not(is_me(j, column)))
        def _():
            greet(j, column)

    for c in wcopies:
        c.wait()
    zero_in = jnp.zeros((pin.shape[0], RANK), BF16)
    w = win[...]
    wip[0] = jnp.concatenate([w, zero_in], axis=1)
    wip[1] = jnp.concatenate([zero_in, w], axis=1)
    zero_out = jnp.zeros((pout.shape[1], RANK), BF16)
    wop[0] = jnp.concatenate([wout[0], zero_out], axis=1)
    wop[1] = jnp.concatenate([zero_out, wout[1]], axis=1)

    on_diagonal = div(d, 2) == t

    @pl.when(on_diagonal)
    def _():
        pl.semaphore_wait(barrier, 52)

    @pl.when(jnp.logical_not(on_diagonal))
    def _():
        pl.semaphore_wait(barrier, 54)

    def step1(r, p, m):
        g = GENS[p][0]
        s = (m + g) % 8 if g == 4 else (
            m + 1 - 2 * (m % 2) if g == 1 else (m // 4) * 4 + 3 - m % 4
        ) if isinstance(m, int) else (
            rem(m + 4, 8) if g == 4 else m + 1 - 2 * rem(m, 2) if g == 1
            else div(m, 4) * 4 + 3 - rem(m, 4)
        )
        return remote(
            acc.at[r, p, m], recv1.at[r, p, s], s1.at[r, p, s], r1.at[r, p, s],
            d, flip(g),
        )

    def span1(p):
        _, g2, g3 = GENS[p]
        return (g2, g2 ^ g3, g3, 0)

    def step2(r, p, k):
        _, g2, g3 = GENS[p]
        return remote(
            acc.at[r, p, (g2, g2 ^ g3)[k]], recv2.at[r, p, k],
            s2.at[r, p, k], r2.at[r, p, k], d, flip(g2),
        )

    def step3(r, p):
        g3 = GENS[p][2]
        return remote(
            acc.at[r, p, g3], recv3.at[r, p], s3.at[r, p], r3.at[r, p], d, flip(g3)
        )

    def sends1(p):
        g1 = GENS[p][0]
        return tuple(s ^ g1 for s in span1(p))

    def begin1(r):
        for k in range(4):
            for p in range(3):
                step1(r, p, sends1(p)[k]).start()

    def begin2(r):
        for p in range(3):
            for k, s in enumerate(span1(p)):
                step1(r, p, s ^ GENS[p][0]).wait_recv()
                acc[r, p, s] = acc[r, p, s] + recv1[r, p, s]
                if k == 1:
                    step2(r, p, 1).start()
                if k == 0:
                    step2(r, p, 0).start()

    def begin3(r):
        for p in range(3):
            g3 = GENS[p][2]
            step2(r, p, 1).wait_recv()
            acc[r, p, g3] = acc[r, p, g3] + recv2[r, p, 1]
            step3(r, p).start()
            step2(r, p, 0).wait_recv()
            acc[r, p, 0] = acc[r, p, 0] + recv2[r, p, 0]

    def end3(r):
        parts = []
        for p in range(3):
            step3(r, p).wait_recv()
            parts.append(acc[r, p, 0] + recv3[r, p])
        return parts

    def drain(r):
        for p in range(3):
            for m in sends1(p):
                step1(r, p, m).wait_send()
            for k in range(2):
                step2(r, p, k).wait_send()
            step3(r, p).wait_send()

    def project(r, j):
        slot = r * 8 + j
        m = 7 - j
        for c in load(r, j):
            c.wait()
        acc[r, 0, m] = jnp.dot(
            xin[slot, :HALF], wip[0], preferred_element_type=F32
        ) + jnp.dot(xin[slot, HALF:], wip[1], preferred_element_type=F32)
        rows = jnp.dot(xgr[slot, 0], wop[0], preferred_element_type=F32) + jnp.dot(
            xgr[slot, 1], wop[1], preferred_element_type=F32
        )
        acc[r, 1, m] = rows[:HALF]
        acc[r, 2, m] = rows[HALF:]

    @pl.loop(0, 8)
    def _(j):
        start_load(1, j)
        project(0, j)
        m = 7 - j
        low = rem(m, 4)

        @pl.when(jnp.logical_or(low == 1, low == 2))
        def _():
            step1(0, 0, m).start()

        @pl.when(low >= 2)
        def _():
            step1(0, 1, m).start()

        @pl.when(m >= 4)
        def _():
            step1(0, 2, m).start()

    def project_some(r, low, high):
        @pl.loop(low, high)
        def _(j):
            if r == 1:
                start_load(2, j)
            project(r, j)

    row64 = lax.broadcasted_iota(jnp.int32, (HALF, BLOCK), 0)
    lane64 = lax.broadcasted_iota(jnp.int32, (HALF, BLOCK), 1)
    left = lane64 < HALF

    def finished(parts, length):
        position = jnp.where(left, row64, row64 + HALF)
        inputs = jnp.where(position < length, parts[0], 0.0)
        turned = pltpu.roll(inputs, HALF, 1)
        twice = jnp.concatenate(
            [jnp.where(left, inputs, turned), jnp.where(left, turned, inputs)], axis=0
        ).astype(BF16)
        outputs = jnp.concatenate(
            [
                jnp.where(row64 < length, parts[1], 0.0),
                jnp.where(row64 + HALF < length, parts[2], 0.0),
            ],
            axis=0,
        )
        return twice, outputs.astype(BF16), outputs.T.astype(BF16)

    def fold(full):
        return jnp.where(left, full[:HALF], full[HALF:])

    def query_sketch(r):
        length = qlen[t * 2 + (r - 1)]
        twice, _, turned = finished(end3(r), length)
        return fold(jnp.dot(turned, twice, preferred_element_type=F32))

    def share(r, m):
        return remote(
            qall.at[r - 1, t], qall.at[r - 1, t], qs.at[r - 1, m], qr.at[r - 1, m], d, flip(m)
        )

    def share_sketch(r):
        qall[r - 1, t] = query_sketch(r)
        for m in range(1, 8):
            share(r, m).start()

    def moment1(m):
        return remote(mloc.at[flip(m)], mrecv1.at[m], ms1.at[m], mr1.at[m], d, flip(m))

    def moment2(j):
        return remote(msum, mrecv2.at[d], ms2.at[j], mr2.at[j], rem(d + j, DP), t)

    def moment3(m):
        return remote(mfull.at[t], mfull.at[t], ms3.at[m], mr3.at[m], d, flip(m))

    def sketch1(m):
        return remote(
            bloc.at[rem(flip(m), 4)], brecv1.at[m], bs1.at[m], br1.at[m], d, flip(m)
        )

    mine = 2 * rem(d, 2) + z

    def sketch2(j):
        return remote(
            bsum, ball.at[mine, x], bs2.at[j], br2.at[mine, x], j, div(d, 2)
        )

    def train_finish():
        length = tlen[z] - x * BLOCK
        twice, outputs, turned = finished(end3(0), length)
        products = jnp.dot(
            turned, jnp.concatenate([outputs, twice], axis=1), preferred_element_type=F32
        )
        ins = lax.dot_general(
            twice, twice, (((0,), (0,)), ((), ())), preferred_element_type=F32
        )
        live = jnp.minimum(jnp.maximum(length, 0), BLOCK).astype(F32)
        mloc[0:4] = fold(products[:, :BLOCK]).reshape(4, 16, BLOCK)
        mloc[4:8] = jnp.where(left, ins[:HALF], live).reshape(4, 16, BLOCK)
        for m in range(1, 8):
            moment1(m).start()
        bloc[...] = fold(products[:, BLOCK:]).reshape(4, 16, BLOCK)
        for m in range(1, 4):
            sketch1(m).start()

    def moments_over_dp():
        total = mloc[t]
        for m in range(1, 8):
            moment1(m).wait_recv()
            total = total + mrecv1[m]
        msum[...] = total
        mrecv2[d] = total

        @pl.loop(1, 16)
        def _(j):
            moment2(j).start()

    def sketches_out():
        total = bloc[x]
        for m in range(1, 4):
            sketch1(m).wait_recv()
            total = total + brecv1[m]
        bsum[...] = total

        @pl.loop(0, 16)
        def _(j):
            me = is_me(j, div(d, 2))

            @pl.when(jnp.logical_not(me))
            def _():
                sketch2(j).start()

            @pl.when(me)
            def _():
                ball[mine, x] = total

    def moments_back():
        @pl.loop(1, 16)
        def _(j):
            moment2(j).wait_recv()

        total = mrecv2[0]
        for j in range(1, 16):
            total = total + mrecv2[j]
        mfull[t] = total
        for m in range(1, 8):
            moment3(m).start()

    def wide(v):
        zero = jnp.zeros_like(v)
        return jnp.concatenate(
            [jnp.where(left, v, zero), jnp.where(left, zero, v)], axis=0
        )

    def product(lhs, rhs):
        lh, ll = split(lhs)
        rh, rl = split(rhs)
        both = jnp.dot(
            jnp.concatenate([lh, ll], axis=1),
            jnp.concatenate(
                [
                    jnp.concatenate([rh, rl], axis=1),
                    jnp.concatenate([rh, jnp.zeros_like(rl)], axis=1),
                ],
                axis=0,
            ),
            preferred_element_type=F32,
        )
        return both[:, :BLOCK] + both[:, BLOCK:]

    exact = functools.partial(
        jnp.dot, precision=lax.Precision.HIGHEST, preferred_element_type=F32
    )

    def invert(matrices):
        eye = jnp.where(rem(lane64, HALF) == row64, 1.0, 0.0).astype(F32)
        first, gains = chebyshev()
        state = [(eye - first * a, first * eye) for a in matrices]
        for g in gains:
            following = []
            for left_over, inverse in state:
                both = product(
                    jnp.concatenate([left_over, inverse], axis=0), wide(left_over)
                )
                following.append(
                    (g * both[:HALF] - (g - 1.0) * eye, g * (inverse + both[HALF:]))
                )
            state = following
        results = []
        for a, (_, inverse) in zip(matrices, state):
            error = exact(a, wide(inverse))
            results.append(2.0 * inverse - exact(inverse, wide(error)))
        return results

    def conditioned():
        for m in range(1, 8):
            moment3(m).wait_recv()
        whole = mfull[...].reshape(2 * HALF, BLOCK)
        outs, ins = whole[:HALF], whole[HALF:]
        live = jnp.max(jnp.where(left, 0.0, ins))
        ins = jnp.where(left, ins, pltpu.roll(ins, HALF, 1))
        diagonal = rem(lane64, HALF) == row64
        left_row = left[0:1]

        def traces(v):
            on = jnp.sum(jnp.where(diagonal, v, 0.0), axis=0, keepdims=True)
            a = jnp.sum(jnp.where(left_row, on, 0.0), axis=1, keepdims=True)
            b = jnp.sum(jnp.where(left_row, 0.0, on), axis=1, keepdims=True)
            return jnp.where(left_row, a, b)

        trace_out, trace_in = traces(outs), traces(ins)
        added = jnp.where(diagonal, DAMPING / RANK, 0.0).astype(F32)
        inv_out, inv_in = invert([outs / trace_out + added, ins / trace_in + added])
        inv_out = inv_out * (live / trace_out)
        inv_in = inv_in * (live / trace_in)

        @pl.loop(0, 16)
        def _(j):
            a, tt = div(j, 8), rem(j, 8)

            @pl.when(jnp.logical_not(is_me(2 * t + a, tt)))
            def _():
                k = 2 * a + div(tt, 4)
                xx = rem(tt, 4)
                remote(
                    bsum, ball.at[k, xx], bs2.at[0], br2.at[k, xx], d, t
                ).wait_recv()

        sketches = jnp.concatenate(
            [ball[e].reshape(HALF, BLOCK) for e in range(4)], axis=1
        )
        wide_out = wide(inv_out)
        twice = jnp.concatenate([sketches, sketches], axis=0)
        solved = []
        for e in range(4):
            solved.append(
                fold(product(wide_out, twice[:, e * BLOCK : (e + 1) * BLOCK]))
            )
        return product(jnp.concatenate(solved, axis=0), wide(inv_in))

    def final(a, tt):
        return remote(
            msg.at[a], fin.at[d], fs.at[a, tt], fr.at[d], 2 * t + a, tt
        )

    def score(weights, scale):
        for r in (1, 2):
            for m in range(1, 8):
                share(r, m).wait_recv()
        queries = qall[...].reshape(16, HALF, BLOCK)
        rows = []
        for e in range(4):
            rows.append(
                jnp.sum(queries * weights[e * HALF : (e + 1) * HALF][None], axis=1)
            )
        rows = jnp.concatenate(rows, axis=0)
        ones = jnp.ones((16, BLOCK), F32)
        sums = lax.dot_general(
            ones, rows, (((1,), (1,)), ((), ())),
            precision=lax.Precision.HIGHEST, preferred_element_type=F32,
        )
        row = lax.broadcasted_iota(jnp.int32, (16, HALF), 0)
        column = lax.broadcasted_iota(jnp.int32, (16, HALF), 1)
        example = div(column, 16)
        kept = jnp.logical_and(
            rem(row, 8) < 2, example == 2 * div(row, 8) + rem(row, 8)
        )
        sums = jnp.where(kept, sums * scale, 0.0)
        at_row = lax.broadcasted_iota(jnp.int32, (HALF, BLOCK), 0)
        at_lane = lax.broadcasted_iota(jnp.int32, (HALF, BLOCK), 1)
        query = 2 * rem(at_row, 8) + rem(div(at_row, 8), 2)
        place = jnp.where(at_lane == rem(d, 8) * 16 + query, 1.0, 0.0).astype(F32)
        msg[...] = exact(sums, place).reshape(2, 8, BLOCK)

        @pl.loop(0, 16)
        def _(j):
            aa, tt = div(j, 8), rem(j, 8)
            me = is_me(2 * t + aa, tt)

            @pl.when(jnp.logical_not(me))
            def _():
                final(aa, tt).start()

            @pl.when(me)
            def _():
                fin[d] = msg[aa]

    project_some(1, 0, 4)
    begin2(0)
    project_some(1, 4, 8)
    begin3(0)
    project_some(2, 0, 4)
    train_finish()
    begin1(1)
    project_some(2, 4, 8)
    moments_over_dp()
    sketches_out()
    begin1(2)
    begin2(1)
    moments_back()
    begin3(1)
    weights = conditioned()
    begin2(2)
    share_sketch(1)
    begin3(2)
    share_sketch(2)
    drain(0)
    drain(1)
    drain(2)
    train_positions, query_positions = tin.shape[1], qin.shape[1]
    score(weights, 1.0 / (RANK * math.sqrt(train_positions * query_positions)))

    for m in range(1, 8):
        moment1(m).wait_send()
        moment3(m).wait_send()
        share(1, m).wait_send()
        share(2, m).wait_send()
    for m in range(1, 4):
        sketch1(m).wait_send()

    @pl.loop(1, 16)
    def _(j):
        moment2(j).wait_send()

    @pl.loop(0, 16)
    def _(j):
        @pl.when(jnp.logical_not(is_me(j, div(d, 2))))
        def _():
            sketch2(j).wait_send()

        aa, tt = div(j, 8), rem(j, 8)

        @pl.when(jnp.logical_not(is_me(2 * t + aa, tt)))
        def _():
            final(aa, tt).wait_send()

        @pl.when(jnp.logical_not(is_me(j, div(d, 2))))
        def _():
            remote(msg.at[0], fin.at[j], fs.at[0, 0], fr.at[j], d, t).wait_recv()

    low, high = fin[0], fin[8]
    for j in range(1, 8):
        low = low + fin[j]
        high = high + fin[j + 8]
    out_ref[:, :BLOCK] = low[:2]
    out_ref[:, BLOCK:] = high[:2]


def on_device(tin, tgr, tlen, qin, qgr, qlen, pin, pout):
    smem = pl.BlockSpec(memory_space=pltpu.SMEM)
    hbm = pl.BlockSpec(memory_space=pl.ANY)
    features, units = pin.shape[0], pout.shape[1]
    piece = (HALF, BLOCK)
    part = (16, BLOCK)
    dma = pltpu.SemaphoreType.DMA
    return pl.pallas_call(
        kernel,
        out_shape=jax.ShapeDtypeStruct((tin.shape[0], DP * qin.shape[0]), F32),
        in_specs=[smem, smem] + [hbm] * 6,
        out_specs=pl.BlockSpec(memory_space=pltpu.VMEM),
        scratch_shapes=[
            pltpu.VMEM((24, BLOCK, features), BF16),
            pltpu.VMEM((24, 2, BLOCK, units), BF16),
            pltpu.VMEM(pin.shape, BF16),
            pltpu.VMEM(pout.shape, BF16),
            pltpu.VMEM((2, features, BLOCK), BF16),
            pltpu.VMEM((2, units, BLOCK), BF16),
            pltpu.VMEM((3, 3, 8) + piece, F32),
            pltpu.VMEM((3, 3, 8) + piece, F32),
            pltpu.VMEM((3, 3, 2) + piece, F32),
            pltpu.VMEM((3, 3) + piece, F32),
            pltpu.VMEM((8,) + part, F32),
            pltpu.VMEM((8,) + part, F32),
            pltpu.VMEM(part, F32),
            pltpu.VMEM((16,) + part, F32),
            pltpu.VMEM((8,) + part, F32),
            pltpu.VMEM((4,) + part, F32),
            pltpu.VMEM((4,) + part, F32),
            pltpu.VMEM(part, F32),
            pltpu.VMEM((4, 4) + part, F32),
            pltpu.VMEM((2, 8) + piece, F32),
            pltpu.VMEM((2, 8, BLOCK), F32),
            pltpu.VMEM((16, 8, BLOCK), F32),
            dma((2, 24)), dma((2,)),
            dma((3, 3, 8)), dma((3, 3, 8)),
            dma((3, 3, 2)), dma((3, 3, 2)),
            dma((3, 3)), dma((3, 3)),
            dma((8,)), dma((8,)), dma((16,)), dma((16,)), dma((8,)), dma((8,)),
            dma((4,)), dma((4,)), dma((16,)), dma((4, 4)),
            dma((2, 8)), dma((2, 8)), dma((2, 8)), dma((16,)),
        ],
        compiler_params=pltpu.CompilerParams(
            collective_id=0, has_side_effects=True, vmem_limit_bytes=48 * 1024 * 1024
        ),
    )(tlen, qlen, tin, tgr, qin, qgr, pin, pout)


def solution(mesh):
    placed = (
        P("dp", None, "tensor"),
        P("dp", None, None, "tensor"),
        P("dp"),
        P("dp", None, "tensor"),
        P("dp", None, None, "tensor"),
        P("dp"),
        P("tensor", None),
        P(None, "tensor", None),
    )
    return jax.shard_map(
        on_device, mesh=mesh, in_specs=placed, out_specs=P("dp", None), check_vma=False
    )
```

time: 245 us -> 76.8 us (0.31)
  the two profiles are of different devices: /device:TPU:0 before, /device:TPU:1 now
where the time goes in v1:
time: 76.8 us; the launch traced here: 76.5 us
  Pallas kernels  69.3 us (90%)
  local copies, waits for them, and re-layouts  7.1 us (9%)
    pallas_call x1, Pallas kernels, on_device(): pl.pallas_call(kernel, out_shape=jax.ShapeDtypeStruct((tin.shape[0], DP *...  69.3 us
    unnamed x11, local copies, waits for them, and re-layouts  7.1 us

profile of v1, /device:TPU:1, one launch (start us, length us, event | category | flops | bytes accessed | tf_op | source)
XLA Modules:
  0.0 76.5 jit_solution(16370758594243182037)
XLA Ops:
  0.0 1.0 %copy.9.pin = bf16[512,64]{1,0:T(8,128)(2,1)S(1)} copy(bf16[512,64]{0,1:T(8,128)(2,1)} %param.14) | data formatting | bytes 131072 | tf_op args[6]
  1.0 1.4 %copy.10.pout = bf16[2,1792,64]{2,1,0:T(8,128)(2,1)S(1)} copy(bf16[2,1792,64]{1,2,0:T(8,128)(2,1)} %param.15) | data formatting | bytes 917504 | tf_op args[7]
  2.4 0.0 copy-start
  2.4 1.6 %copy-done = bf16[16,128,512]{2,1,0:T(8,128)(2,1)S(1)} copy-done((bf16[16,128,512]{2,1,0:T(8,128)(2,1)S(1)}, bf16[16,128,512]{2,1,0:T(8,128)(2,1)}, u32[]{:S(2)}) %copy-start) | copy-done | bytes 2097176
  4.0 0.0 copy-start.1
  4.0 1.2 %copy-done.1 = bf16[2,512,512]{2,1,0:T(8,128)(2,1)S(1)} copy-done((bf16[2,512,512]{2,1,0:T(8,128)(2,1)S(1)}, bf16[2,512,512]{2,1,0:T(8,128)(2,1)}, u32[]{:S(2)}) %copy-start.1) | copy-done | bytes 1048600
  5.2 0.0 copy-start.2
  5.2 0.7 copy-done.2
  5.9 0.0 copy-start.3
  5.9 0.7 copy-done.3
  6.5 69.3 %shard_map.82 = f32[2,256]{1,0:T(2,128)S(1)} custom-call(s32[2]{0:T(128)S(1)} %copy-done.2, s32[16]{0:T(128)S(1)} %copy-done.3, bf16[2,512,512]{2,1,0:T(8,128)(2,1)S(1)} %copy-done.1, bf16[2,2,512,1792]{3,2,1,0:T(8,128)(2,1)} %tgr.1, bf16[16,128,512]{2,1,0:T(8,128)(2,1)S(1)} %copy-done, bf16[16,2,128,1792]{3,2,1,0:T(8,128)(2,1)} %qgr.1, ...), custom_call_target="tpu_custom_call" | custom-call | tf_op jit(solution)/shard_map/pallas_call | solution.py:597
  75.9 0.6 copy.12
Async XLA Ops:
  2.4 1.6 %copy-start = (bf16[16,128,512]{2,1,0:T(8,128)(2,1)S(1)}, bf16[16,128,512]{2,1,0:T(8,128)(2,1)}, u32[]{:S(2)}) copy-start(bf16[16,128,512]{2,1,0:T(8,128)(2,1)} %qin.1) | copy-start | bytes 6291460
  4.0 1.2 %copy-start.1 = (bf16[2,512,512]{2,1,0:T(8,128)(2,1)S(1)}, bf16[2,512,512]{2,1,0:T(8,128)(2,1)}, u32[]{:S(2)}) copy-start(bf16[2,512,512]{2,1,0:T(8,128)(2,1)} %tin.1) | copy-start | bytes 3145732
  5.2 0.7 copy-start.2
  5.9 0.7 copy-start.3

commit v2 on v0

v2 whole, which is shorter than its diff:
```python
import contextlib
import functools
import math

import jax
import jax.numpy as jnp
from jax import lax
from jax.experimental import pallas as pl
from jax.experimental.pallas import tpu as pltpu
from jax.sharding import PartitionSpec as P

MESH = pl.DeviceIdType.MESH
SCOPES = False


def scope(name):
    return jax.named_scope(name) if SCOPES else contextlib.nullcontext()


F32 = jnp.float32
BF16 = jnp.bfloat16
DAMPING = 0.1
RANK = 64
BLOCK = 128
HALF = 64
DP = 16
DOUBLINGS = 7
GENS = ((1, 3, 4), (3, 4, 1), (4, 1, 3))


def chebyshev():
    low = DAMPING / RANK
    high = 1.0 + low
    angle = math.acosh((high + low) / (high - low))
    gains = []
    n = 1
    for _ in range(DOUBLINGS):
        gains.append(2.0 * math.cosh(n * angle) ** 2 / math.cosh(2 * n * angle))
        n *= 2
    return 2.0 / (high + low), gains


def rem(a, b):
    return lax.rem(a, jnp.int32(b))


def div(a, b):
    return lax.div(a, jnp.int32(b))


def split(v):
    high = v.astype(BF16)
    return high, (v - high.astype(F32)).astype(BF16)


def kernel(
    tlen_hbm, qlen_hbm, tin, tgr, qin, qgr, pin, pout, out_ref,
    tlen, qlen, xin, xgr, wip, wop, acc, got, got2, got3, part, msum, bsum, qall, msg, fin,
    wsem, isem, gsem, send, recv1, recv2, recv3, msend, mrecv, bsend, brecv, qsend, qrecv, fsend, frecv,
):
    d = lax.axis_index("dp").astype(jnp.int32)
    t = lax.axis_index("tensor").astype(jnp.int32)
    z, x = div(t, 4), rem(t, 4)
    column = div(d, 2)
    on_diagonal = column == t

    def flip(m):
        m = jnp.int32(m)
        mx, mz = rem(m, 4), div(m, 4)
        low = rem(x + mx, 2)
        high = rem(div(x, 2) + div(mx, 2), 2)
        return rem(z + mz, 2) * 4 + high * 2 + low

    def remote(src, dst, ssem, rsem, dd, tt):
        return pltpu.make_async_remote_copy(
            src_ref=src, dst_ref=dst, send_sem=ssem, recv_sem=rsem,
            device_id=(dd, tt), device_id_type=MESH,
        )

    def wait(ref, sem):
        pltpu.make_async_copy(ref, ref, sem).wait()

    def is_me(dd, tt):
        return jnp.logical_and(dd == d, tt == t)

    def unless(condition):
        return pl.when(jnp.logical_not(condition))

    def load(pair, query):
        sem = rem(pair, 4)
        m = 7 - 2 * sem
        for h in range(2):
            item = flip(m - h)
            if query:
                q = item * 2 + (div(pair, 4) - 1)
                a, b = qin.at[q], qgr.at[q]
            else:
                rows = pl.ds(pl.multiple_of(rem(item, 4) * BLOCK, BLOCK), BLOCK)
                e = div(item, 4)
                a, b = tin.at[e, rows, :], tgr.at[e, :, rows, :]
            to = pl.ds(h * BLOCK, BLOCK)
            pltpu.make_async_copy(a, xin.at[pair, to], isem.at[sem]).start()
            pltpu.make_async_copy(b, xgr.at[pair, :, to], gsem.at[sem]).start()

    with scope("start_loads"):
        pltpu.make_async_copy(pin, wip.at[0, :RANK], wsem.at[0]).start()
        pltpu.make_async_copy(pin, wip.at[1, RANK:], wsem.at[0]).start()
        pltpu.make_async_copy(pout.at[0], wop.at[0, :RANK], wsem.at[1]).start()
        pltpu.make_async_copy(pout.at[1], wop.at[1, RANK:], wsem.at[1]).start()

        @pl.loop(0, 4)
        def _(pair):
            load(pair, False)

        lengths = (
            pltpu.make_async_copy(tlen_hbm, tlen, wsem.at[2]),
            pltpu.make_async_copy(qlen_hbm, qlen, wsem.at[3]),
        )
        for c in lengths:
            c.start()

    barrier = pltpu.get_barrier_semaphore()

    def greet(dd, tt):
        pl.semaphore_signal(barrier, inc=1, device_id=(dd, tt), device_id_type=MESH)

    with scope("greet"):

        @pl.loop(1, 8)
        def _(m):
            greet(d, flip(m))

        @pl.loop(1, 16)
        def _(j):
            greet(rem(d + j, DP), t)

        @pl.loop(0, 16)
        def _(j):
            dd, tt = t * 2 + div(j, 8), rem(j, 8)

            @unless(is_me(dd, tt))
            def _():
                greet(dd, tt)

            @unless(is_me(j, column))
            def _():
                greet(j, column)

    with scope("weights"):
        wip[0, RANK:] = jnp.zeros(pin.shape, BF16)
        wip[1, :RANK] = jnp.zeros(pin.shape, BF16)
        wop[0, RANK:] = jnp.zeros(pout.shape[1:], BF16)
        wop[1, :RANK] = jnp.zeros(pout.shape[1:], BF16)
        wait(wip.at[0], wsem.at[0])
        wait(wop.at[0], wsem.at[1])
        for c in lengths:
            c.wait()

    with scope("barrier_wait"):

        @pl.when(on_diagonal)
        def _():
            pl.semaphore_wait(barrier, 52)

        @unless(on_diagonal)
        def _():
            pl.semaphore_wait(barrier, 54)

    def rows_of(p):
        return slice(HALF * p, HALF * (p + 1))

    def piece(r, p, m):
        return acc.at[r * 8 + m, rows_of(p)]

    def first(r, p, m, s):
        return remote(
            piece(r, p, m), got.at[r * 8 + s, rows_of(p)],
            send, recv1.at[r, p], d, flip(GENS[p][0]),
        )

    def times(rows, turned):
        return lax.dot_general(
            rows, turned, (((1,), (1,)), ((), ())), preferred_element_type=F32
        )

    def project(pair):
        r, sem = div(pair, 4), rem(pair, 4)
        m = 7 - 2 * sem
        wait(xin.at[pair], isem.at[sem])
        wait(xgr.at[pair], gsem.at[sem])

        @pl.when(pair < 8)
        def _():
            load(pair + 4, True)

        rows = xin[pair]
        low = jnp.concatenate([rows[:HALF], rows[BLOCK : BLOCK + HALF]], axis=0)
        high = jnp.concatenate([rows[HALF:BLOCK], rows[BLOCK + HALF :]], axis=0)
        ins = times(low, wip[0]) + times(high, wip[1])
        outs = times(xgr[pair, 0], wop[0]) + times(xgr[pair, 1], wop[1])
        for h in range(2):
            slot = r * 8 + m - h
            acc[slot, :HALF] = ins[h * HALF : (h + 1) * HALF]
            acc[slot, HALF:] = outs[h * BLOCK : (h + 1) * BLOCK]

        @pl.when(r == 0)
        def _():
            for h in range(2):
                item = m - h
                low = rem(item, 4)
                sent = (jnp.logical_or(low == 1, low == 2), low >= 2, item >= 4)
                after = (
                    item + 1 - 2 * rem(item, 2),
                    item - low + 3 - low,
                    item - 4,
                )
                for p in range(3):

                    @pl.when(sent[p])
                    def _(p=p):
                        first(0, p, item, after[p]).start()

    def project_pairs(low, high):
        pl.loop(low, high)(project)

    def halve1(r):
        for k in range(4):
            for p, (g1, g2, g3) in enumerate(GENS):
                s = (g2, g2 ^ g3, g3, 0)[k]
                first(r, p, s ^ g1, s).start()

    def add(r, p, s, ref):
        rows = rows_of(p)
        acc[r * 8 + s, rows] = acc[r * 8 + s, rows] + ref[...]

    def halve2(r):
        for p, (_, g2, g3) in enumerate(GENS):
            wait(qall.at[pl.ds(0, 4)], recv1.at[r, p])
            for k, s in enumerate((g2, g2 ^ g3)):
                add(r, p, s, got.at[r * 8 + s, rows_of(p)])
                remote(
                    piece(r, p, s), got2.at[r, p, k],
                    send, recv2.at[r, p], d, flip(g2),
                ).start()
        for p, (_, _, g3) in enumerate(GENS):
            for s in (g3, 0):
                add(r, p, s, got.at[r * 8 + s, rows_of(p)])

    def halve3(r):
        for p, (_, _, g3) in enumerate(GENS):
            wait(qall.at[pl.ds(0, 2)], recv2.at[r, p])
            add(r, p, g3, got2.at[r, p, 1])
            remote(
                piece(r, p, g3), got3.at[r, p], send, recv3.at[r, p], d, flip(g3)
            ).start()
        for p in range(3):
            add(r, p, 0, got2.at[r, p, 0])

    def halved(r):
        for p in range(3):
            wait(qall.at[0], recv3.at[r, p])
        return acc[r * 8] + jnp.concatenate([got3[r, p] for p in range(3)], axis=0)

    row64 = lax.broadcasted_iota(jnp.int32, (HALF, BLOCK), 0)
    lane64 = lax.broadcasted_iota(jnp.int32, (HALF, BLOCK), 1)
    left = lane64 < HALF

    def finished(total, length):
        position = jnp.where(left, row64, row64 + HALF)
        inputs = jnp.where(position < length, total[:HALF], 0.0)
        turned = pltpu.roll(inputs, HALF, 1)
        twice = jnp.concatenate(
            [jnp.where(left, inputs, turned), jnp.where(left, turned, inputs)], axis=0
        ).astype(BF16)
        outputs = jnp.concatenate(
            [
                jnp.where(row64 < length, total[HALF:BLOCK], 0.0),
                jnp.where(row64 + HALF < length, total[BLOCK:], 0.0),
            ],
            axis=0,
        )
        return twice, outputs.astype(BF16), outputs.T.astype(BF16)

    def fold(full):
        return jnp.where(left, full[:HALF], full[HALF:])

    def query_sketch(total, r):
        length = qlen[t * 2 + (r - 1)]
        twice, _, turned = finished(total, length)
        return fold(jnp.dot(turned, twice, preferred_element_type=F32))

    def share(r, m):
        mine = qall.at[(r - 1) * 8 + t]
        return remote(mine, mine, qsend, qrecv.at[r - 1], d, flip(m))

    def share_sketch(r):
        with scope("halved"):
            total = halved(r)
        qall[(r - 1) * 8 + t] = query_sketch(total, r)
        for m in range(1, 8):
            share(r, m).start()

    def moment1(m):
        return remote(part.at[flip(m)], part.at[8 + m], msend, mrecv.at[0], d, flip(m))

    def moment2(j):
        return remote(msum, part.at[16 + d], msend, mrecv.at[1], rem(d + j, DP), t)

    def moment3(m):
        return remote(
            part.at[32 + t], part.at[32 + t], msend, mrecv.at[2], d, flip(m)
        )

    def sketch1(m):
        return remote(
            part.at[40 + rem(flip(m), 4)], part.at[44 + m], bsend, brecv.at[0], d, flip(m)
        )

    my_quarter = 48 + 4 * (2 * rem(d, 2) + z) + x

    def sketch2(j):
        return remote(bsum, part.at[my_quarter], bsend, brecv.at[1], j, column)

    def train_finish():
        with scope("halved"):
            total = halved(0)
        length = tlen[z] - x * BLOCK
        twice, outputs, turned = finished(total, length)
        products = jnp.dot(
            turned, jnp.concatenate([outputs, twice], axis=1), preferred_element_type=F32
        )
        ins = lax.dot_general(
            twice, twice, (((0,), (0,)), ((), ())), preferred_element_type=F32
        )
        live = jnp.minimum(jnp.maximum(length, 0), BLOCK).astype(F32)
        part[0:4] = fold(products[:, :BLOCK]).reshape(4, 16, BLOCK)
        part[4:8] = jnp.where(left, ins[:HALF], live).reshape(4, 16, BLOCK)
        for m in range(7, 0, -1):
            moment1(m).start()
        part[40:44] = fold(products[:, BLOCK:]).reshape(4, 16, BLOCK)
        for m in range(1, 4):
            sketch1(m).start()

    def moments_over_dp():
        wait(part.at[pl.ds(9, 7)], mrecv.at[0])
        total = part[t]
        for m in range(1, 8):
            total = total + part[8 + m]
        msum[...] = total
        part[16 + d] = total

        @pl.loop(1, 16)
        def _(j):
            moment2(j).start()

    def sketches_out():
        wait(part.at[pl.ds(45, 3)], brecv.at[0])
        total = part[40 + x]
        for m in range(1, 4):
            total = total + part[44 + m]
        bsum[...] = total

        @pl.loop(0, 16)
        def _(j):
            me = is_me(j, column)

            @unless(me)
            def _():
                sketch2(j).start()

            @pl.when(me)
            def _():
                part[my_quarter] = total

    def moments_back():
        wait(part.at[pl.ds(16, 15)], mrecv.at[1])
        total = part[16]
        for j in range(1, 16):
            total = total + part[16 + j]
        part[32 + t] = total
        for m in range(7, 0, -1):
            moment3(m).start()

    def wide(v):
        zero = jnp.zeros_like(v)
        return jnp.concatenate(
            [jnp.where(left, v, zero), jnp.where(left, zero, v)], axis=0
        )

    def product(lhs, rhs):
        lh, ll = split(lhs)
        rh, rl = split(rhs)
        both = jnp.dot(
            jnp.concatenate([lh, ll], axis=1),
            jnp.concatenate(
                [
                    jnp.concatenate([rh, rl], axis=1),
                    jnp.concatenate([rh, jnp.zeros_like(rl)], axis=1),
                ],
                axis=0,
            ),
            preferred_element_type=F32,
        )
        return both[:, : rhs.shape[1]] + both[:, rhs.shape[1] :]

    exact = functools.partial(
        jnp.dot, precision=lax.Precision.HIGHEST, preferred_element_type=F32
    )

    def invert(matrices):
        eye = jnp.where(rem(lane64, HALF) == row64, 1.0, 0.0).astype(F32)
        first, gains = chebyshev()
        state = [(eye - first * a, first * eye) for a in matrices]
        for g in gains:
            following = []
            for left_over, inverse in state:
                both = product(
                    jnp.concatenate([left_over, inverse], axis=0), wide(left_over)
                )
                following.append(
                    (g * both[:HALF] - (g - 1.0) * eye, g * (inverse + both[HALF:]))
                )
            state = following
        results = []
        for a, (_, inverse) in zip(matrices, state):
            error = exact(a, wide(inverse))
            results.append(2.0 * inverse - exact(inverse, wide(error)))
        return results

    def inverses():
        with scope("wait_moment3"):
            wait(part.at[pl.ds(32, 7)], mrecv.at[2])
        whole = part[32:40].reshape(2 * HALF, BLOCK)
        outs, ins = whole[:HALF], whole[HALF:]
        live = jnp.max(jnp.where(left, 0.0, ins))
        ins = jnp.where(left, ins, pltpu.roll(ins, HALF, 1))
        diagonal = rem(lane64, HALF) == row64
        left_row = left[0:1]

        def traces(v):
            on = jnp.sum(jnp.where(diagonal, v, 0.0), axis=0, keepdims=True)
            a = jnp.sum(jnp.where(left_row, on, 0.0), axis=1, keepdims=True)
            b = jnp.sum(jnp.where(left_row, 0.0, on), axis=1, keepdims=True)
            return jnp.where(left_row, a, b)

        trace_out, trace_in = traces(outs), traces(ins)
        added = jnp.where(diagonal, DAMPING / RANK, 0.0).astype(F32)
        inv_out, inv_in = invert([outs / trace_out + added, ins / trace_in + added])
        return inv_out * (live / trace_out), inv_in * (live / trace_in)

    def diagonal_or_not(f):
        pl.when(on_diagonal)(functools.partial(f, 15))
        unless(on_diagonal)(functools.partial(f, 16))

    def solve(inv_out, inv_in):
        with scope("wait_sketches"):
            diagonal_or_not(lambda n: wait(part.at[pl.ds(48, n)], brecv.at[1]))
        wide_out = wide(inv_out)
        solved = []
        for e in range(4):
            sketch = part[48 + 4 * e : 52 + 4 * e].reshape(HALF, BLOCK)
            solved.append(
                fold(product(wide_out, jnp.concatenate([sketch, sketch], axis=0)))
            )
        return product(jnp.concatenate(solved, axis=0), wide(inv_in))

    def final(a, tt):
        return remote(msg.at[a], fin.at[d], fsend, frecv, 2 * t + a, tt)

    def score(weights, scale):
        with scope("wait_share"):
            for r in range(2):
                wait(qall.at[pl.ds(r * 8, 7)], qrecv.at[r])
        queries = qall[...]
        rows = []
        for e in range(4):
            rows.append(
                jnp.sum(queries * weights[e * HALF : (e + 1) * HALF][None], axis=1)
            )
        rows = jnp.concatenate(rows, axis=0)
        ones = jnp.ones((16, BLOCK), F32)
        sums = lax.dot_general(
            ones, rows, (((1,), (1,)), ((), ())),
            precision=lax.Precision.HIGHEST, preferred_element_type=F32,
        )
        row = lax.broadcasted_iota(jnp.int32, (16, HALF), 0)
        lane = lax.broadcasted_iota(jnp.int32, (16, HALF), 1)
        example = div(lane, 16)
        kept = jnp.logical_and(
            rem(row, 8) < 2, example == 2 * div(row, 8) + rem(row, 8)
        )
        sums = jnp.where(kept, sums * scale, 0.0)
        at_row = lax.broadcasted_iota(jnp.int32, (HALF, BLOCK), 0)
        at_lane = lax.broadcasted_iota(jnp.int32, (HALF, BLOCK), 1)
        query = 2 * rem(at_row, 8) + rem(div(at_row, 8), 2)
        place = jnp.where(at_lane == rem(d, 8) * 16 + query, 1.0, 0.0).astype(F32)
        msg[...] = exact(sums, place).reshape(2, 8, BLOCK)

        @pl.loop(0, 16)
        def _(j):
            a, tt = div(j, 8), rem(j, 8)
            me = is_me(2 * t + a, tt)

            @unless(me)
            def _():
                final(a, tt).start()

            @pl.when(me)
            def _():
                fin[d] = msg[a]

    def do(name, f, *args):
        with scope(name):
            return f(*args)

    do("project_0", project_pairs, 0, 4)
    do("project_1", project_pairs, 4, 8)
    do("halve2_0", halve2, 0)
    do("halve1_1", halve1, 1)
    do("project_2a", project_pairs, 8, 11)
    do("halve3_0", halve3, 0)
    do("project_2b", project_pairs, 11, 12)
    do("train_finish", train_finish)
    do("halve2_1", halve2, 1)
    do("halve1_2", halve1, 2)
    do("moments_over_dp", moments_over_dp)
    do("halve3_1", halve3, 1)
    do("halve2_2", halve2, 2)
    do("sketches_out", sketches_out)
    do("share_1", share_sketch, 1)
    do("moments_back", moments_back)
    do("halve3_2", halve3, 2)
    do("share_2", share_sketch, 2)
    inv_out, inv_in = do("inverses", inverses)
    weights = do("solve", solve, inv_out, inv_in)
    train_positions, query_positions = tin.shape[1], qin.shape[1]
    scale = 1.0 / (RANK * math.sqrt(train_positions * query_positions))
    do("score", score, weights, scale)

    with scope("drain"):
        wait(acc.at[pl.ds(0, 21)], send)
        wait(part.at[pl.ds(0, 29)], msend)
        diagonal_or_not(lambda n: wait(part.at[pl.ds(0, n + 3)], bsend))
        wait(qall.at[pl.ds(0, 14)], qsend)
    with scope("final_wait"):
        diagonal_or_not(lambda n: wait(fin.at[pl.ds(0, n)], frecv))
    with scope("final_drain"):
        diagonal_or_not(lambda n: wait(fin.at[pl.ds(0, n)], fsend))
    low, high = fin[0], fin[8]
    for j in range(1, 8):
        low = low + fin[j]
        high = high + fin[j + 8]
    out_ref[:, :BLOCK] = low[:2]
    out_ref[:, BLOCK:] = high[:2]


def on_device(tin, tgr, tlen, qin, qgr, qlen, pin, pout):
    hbm = pl.BlockSpec(memory_space=pltpu.HBM)
    features, units = pin.shape[0], pout.shape[1]
    dma = pltpu.SemaphoreType.DMA
    return pl.pallas_call(
        kernel,
        out_shape=jax.ShapeDtypeStruct((tin.shape[0], DP * qin.shape[0]), F32),
        in_specs=[hbm] * 8,
        out_specs=pl.BlockSpec(memory_space=pltpu.VMEM),
        scratch_shapes=[
            pltpu.SMEM(tlen.shape, jnp.int32),
            pltpu.SMEM(qlen.shape, jnp.int32),
            pltpu.VMEM((12, 2 * BLOCK, features), BF16),
            pltpu.VMEM((12, 2, 2 * BLOCK, units), BF16),
            pltpu.VMEM((2, BLOCK, features), BF16),
            pltpu.VMEM((2, BLOCK, units), BF16),
            pltpu.VMEM((24, HALF + BLOCK, BLOCK), F32),
            pltpu.VMEM((24, HALF + BLOCK, BLOCK), F32),
            pltpu.VMEM((3, 3, 2, HALF, BLOCK), F32),
            pltpu.VMEM((3, 3, HALF, BLOCK), F32),
            pltpu.VMEM((64, 16, BLOCK), F32),
            pltpu.VMEM((16, BLOCK), F32),
            pltpu.VMEM((16, BLOCK), F32),
            pltpu.VMEM((16, HALF, BLOCK), F32),
            pltpu.VMEM((2, 8, BLOCK), F32),
            pltpu.VMEM((16, 8, BLOCK), F32),
            dma((4,)), dma((4,)), dma((4,)),
            dma, dma((3, 3)), dma((3, 3)), dma((3, 3)), dma, dma((3,)), dma, dma((2,)), dma, dma((2,)), dma, dma,
        ],
        compiler_params=pltpu.CompilerParams(
            collective_id=0, has_side_effects=True, vmem_limit_bytes=56 * 1024 * 1024
        ),
    )(tlen, qlen, tin, tgr, qin, qgr, pin.T, pout.transpose(0, 2, 1))


def solution(mesh):
    placed = (
        P("dp", None, "tensor"),
        P("dp", None, None, "tensor"),
        P("dp"),
        P("dp", None, "tensor"),
        P("dp", None, None, "tensor"),
        P("dp"),
        P("tensor", None),
        P(None, "tensor", None),
    )
    return jax.shard_map(
        on_device, mesh=mesh, in_specs=placed, out_specs=P("dp", None), check_vma=False
    )
```

time: 245 us -> 57.9 us (0.24)
  the two profiles are of different devices: /device:TPU:0 before, /device:TPU:1 now
where the time goes in v2:
time: 57.9 us; the launch traced here: 57.7 us
  Pallas kernels  56.5 us (98%)
  local copies, waits for them, and re-layouts  1.26 us (2%)
    pallas_call x1, Pallas kernels, on_device(): pl.pallas_call(kernel, out_shape=jax.ShapeDtypeStruct((tin.shape[0], DP *...  56.5 us
    unnamed x1, local copies, waits for them, and re-layouts  1.26 us

profile of v2, /device:TPU:1, one launch (start us, length us, event | category | flops | bytes accessed | tf_op | source)
XLA Modules:
  0.0 57.7 jit_solution(2625663991613862954)
XLA Ops:
  0.0 56.5 %shard_map.82 = f32[2,256]{1,0:T(2,128)} custom-call(s32[2]{0:T(128)} %tlen_hbm.1, s32[16]{0:T(128)} %qlen_hbm.1, bf16[2,512,512]{2,1,0:T(8,128)(2,1)} %tin.1, bf16[2,2,512,1792]{3,2,1,0:T(8,128)(2,1)} %tgr.1, bf16[16,128,512]{2,1,0:T(8,128)(2,1)} %qin.1, bf16[16,2,128,1792]{3,2,1,0:T(8,128)(2,1)} %qgr.1, bf16[64,512]{1,0:T(8,128)(2,1)} %bitcast.3, ...), custom_call_target="tpu_custom_call" | custom-call | tf_op jit(solution)/shard_map/pallas_call | solution.py:561
  56.5 1.3 %copy.10 = f32[2,256]{1,0:T(2,128)} copy(f32[2,256]{1,0:T(2,128)} %shard_map.82) | data formatting | bytes 4096

commit v3 on v2

--- a/solution.py
+++ b/solution.py
@@ -31,13 +31,7 @@
 def chebyshev():
     low = DAMPING / RANK
     high = 1.0 + low
-    angle = math.acosh((high + low) / (high - low))
-    gains = []
-    n = 1
-    for _ in range(DOUBLINGS):
-        gains.append(2.0 * math.cosh(n * angle) ** 2 / math.cosh(2 * n * angle))
-        n *= 2
-    return 2.0 / (high + low), gains
+    return 2.0 / (high + low), (high + low) / (high - low)
 
 
 def rem(a, b):
@@ -61,8 +55,8 @@
     d = lax.axis_index("dp").astype(jnp.int32)
     t = lax.axis_index("tensor").astype(jnp.int32)
     z, x = div(t, 4), rem(t, 4)
-    column = div(d, 2)
-    on_diagonal = column == t
+    column = div(d, 4)
+    on_diagonal = column == x
 
     def flip(m):
         m = jnp.int32(m)
@@ -100,7 +94,8 @@
                 a, b = tin.at[e, rows, :], tgr.at[e, :, rows, :]
             to = pl.ds(h * BLOCK, BLOCK)
             pltpu.make_async_copy(a, xin.at[pair, to], isem.at[sem]).start()
-            pltpu.make_async_copy(b, xgr.at[pair, :, to], gsem.at[sem]).start()
+            to = pl.ds((pair * 2 + h) * BLOCK, BLOCK)
+            pltpu.make_async_copy(b, xgr.at[:, to], gsem.at[sem]).start()
 
     with scope("start_loads"):
         pltpu.make_async_copy(pin, wip.at[0, :RANK], wsem.at[0]).start()
@@ -134,17 +129,13 @@
         def _(j):
             greet(rem(d + j, DP), t)
 
-        @pl.loop(0, 16)
+        @pl.loop(0, 32)
         def _(j):
-            dd, tt = t * 2 + div(j, 8), rem(j, 8)
+            dd, tt = div(j, 2), rem(j, 2) * 4 + column
 
             @unless(is_me(dd, tt))
             def _():
                 greet(dd, tt)
-
-            @unless(is_me(j, column))
-            def _():
-                greet(j, column)
 
     with scope("weights"):
         wip[0, RANK:] = jnp.zeros(pin.shape, BF16)
@@ -156,16 +147,6 @@
         for c in lengths:
             c.wait()
 
-    with scope("barrier_wait"):
-
-        @pl.when(on_diagonal)
-        def _():
-            pl.semaphore_wait(barrier, 52)
-
-        @unless(on_diagonal)
-        def _():
-            pl.semaphore_wait(barrier, 54)
-
     def rows_of(p):
         return slice(HALF * p, HALF * (p + 1))
 
@@ -183,45 +164,43 @@
             rows, turned, (((1,), (1,)), ((), ())), preferred_element_type=F32
         )
 
-    def project(pair):
-        r, sem = div(pair, 4), rem(pair, 4)
-        m = 7 - 2 * sem
-        wait(xin.at[pair], isem.at[sem])
-        wait(xgr.at[pair], gsem.at[sem])
-
-        @pl.when(pair < 8)
+    def project(four):
+        pairs = (2 * four, 2 * four + 1)
+        for pair in pairs:
+            sem = rem(pair, 4)
+            wait(xin.at[pair], isem.at[sem])
+            wait(xgr.at[:, pl.ds(pair * 2 * BLOCK, 2 * BLOCK)], gsem.at[sem])
+
+        @pl.when(four < 4)
         def _():
-            load(pair + 4, True)
-
-        rows = xin[pair]
-        low = jnp.concatenate([rows[:HALF], rows[BLOCK : BLOCK + HALF]], axis=0)
-        high = jnp.concatenate([rows[HALF:BLOCK], rows[BLOCK + HALF :]], axis=0)
-        ins = times(low, wip[0]) + times(high, wip[1])
-        outs = times(xgr[pair, 0], wop[0]) + times(xgr[pair, 1], wop[1])
-        for h in range(2):
-            slot = r * 8 + m - h
-            acc[slot, :HALF] = ins[h * HALF : (h + 1) * HALF]
-            acc[slot, HALF:] = outs[h * BLOCK : (h + 1) * BLOCK]
-
-        @pl.when(r == 0)
-        def _():
-            for h in range(2):
-                item = m - h
-                low = rem(item, 4)
-                sent = (jnp.logical_or(low == 1, low == 2), low >= 2, item >= 4)
-                after = (
-                    item + 1 - 2 * rem(item, 2),
-                    item - low + 3 - low,
-                    item - 4,
-                )
-                for p in range(3):
-
-                    @pl.when(sent[p])
-                    def _(p=p):
-                        first(0, p, item, after[p]).start()
-
-    def project_pairs(low, high):
-        pl.loop(low, high)(project)
+            for pair in pairs:
+                load(pair + 4, True)
+
+        def rows(start):
+            return jnp.concatenate(
+                [
+                    xin[pair, h * BLOCK + start : h * BLOCK + start + HALF]
+                    for pair in pairs
+                    for h in range(2)
+                ],
+                axis=0,
+            )
+
+        ins = times(rows(0), wip[0]) + times(rows(HALF), wip[1])
+        units = pl.ds(four * 4 * BLOCK, 4 * BLOCK)
+        outs = times(xgr[0, units], wop[0]) + times(xgr[1, units], wop[1])
+        for i in range(4):
+            slot = div(four, 2) * 8 + 7 - 4 * rem(four, 2) - i
+            acc[slot, :HALF] = ins[i * HALF : (i + 1) * HALF]
+            acc[slot, HALF:] = outs[i * BLOCK : (i + 1) * BLOCK]
+
+    def send_items(*which):
+        for p, m in which:
+            first(0, p, m, m ^ GENS[p][0]).start()
+
+    def everyone_is_here():
+        pl.when(on_diagonal)(lambda: pl.semaphore_wait(barrier, 53))
+        unless(on_diagonal)(lambda: pl.semaphore_wait(barrier, 54))
 
     def halve1(r):
         for k in range(4):
@@ -240,7 +219,7 @@
                 add(r, p, s, got.at[r * 8 + s, rows_of(p)])
                 remote(
                     piece(r, p, s), got2.at[r, p, k],
-                    send, recv2.at[r, p], d, flip(g2),
+                    send, recv2.at[r % 2, p], d, flip(g2),
                 ).start()
         for p, (_, _, g3) in enumerate(GENS):
             for s in (g3, 0):
@@ -248,17 +227,17 @@
 
     def halve3(r):
         for p, (_, _, g3) in enumerate(GENS):
-            wait(qall.at[pl.ds(0, 2)], recv2.at[r, p])
+            wait(qall.at[pl.ds(0, 2)], recv2.at[r % 2, p])
             add(r, p, g3, got2.at[r, p, 1])
             remote(
-                piece(r, p, g3), got3.at[r, p], send, recv3.at[r, p], d, flip(g3)
+                piece(r, p, g3), got3.at[r, p], send, recv3.at[r % 2, p], d, flip(g3)
             ).start()
         for p in range(3):
             add(r, p, 0, got2.at[r, p, 0])
 
     def halved(r):
         for p in range(3):
-            wait(qall.at[0], recv3.at[r, p])
+            wait(qall.at[0], recv3.at[r % 2, p])
         return acc[r * 8] + jnp.concatenate([got3[r, p] for p in range(3)], axis=0)
 
     row64 = lax.broadcasted_iota(jnp.int32, (HALF, BLOCK), 0)
@@ -290,14 +269,14 @@
         return fold(jnp.dot(turned, twice, preferred_element_type=F32))
 
     def share(r, m):
-        mine = qall.at[(r - 1) * 8 + t]
+        mine = qall.at[(r - 1) * 4 + x]
         return remote(mine, mine, qsend, qrecv.at[r - 1], d, flip(m))
 
     def share_sketch(r):
         with scope("halved"):
             total = halved(r)
-        qall[(r - 1) * 8 + t] = query_sketch(total, r)
-        for m in range(1, 8):
+        qall[(r - 1) * 4 + x] = query_sketch(total, r)
+        for m in (2, 1, 3):
             share(r, m).start()
 
     def moment1(m):
@@ -316,10 +295,14 @@
             part.at[40 + rem(flip(m), 4)], part.at[44 + m], bsend, brecv.at[0], d, flip(m)
         )
 
-    my_quarter = 48 + 4 * (2 * rem(d, 2) + z) + x
-
     def sketch2(j):
-        return remote(bsum, part.at[my_quarter], bsend, brecv.at[1], j, column)
+        return remote(bsum, part.at[48 + d], bsend, brecv.at[1], rem(d + j, DP), t)
+
+    def sketch3(m):
+        return remote(
+            part.at[pl.ds(48 + 4 * rem(flip(m), 4), 4)], part.at[pl.ds(64 + 4 * t, 4)],
+            bsend, brecv.at[2], d, flip(m),
+        )
 
     def train_finish():
         with scope("halved"):
@@ -359,18 +342,17 @@
         for m in range(1, 4):
             total = total + part[44 + m]
         bsum[...] = total
-
-        @pl.loop(0, 16)
+        part[48 + d] = total
+
+        @pl.loop(1, 16)
         def _(j):
-            me = is_me(j, column)
-
-            @unless(me)
-            def _():
-                sketch2(j).start()
-
-            @pl.when(me)
-            def _():
-                part[my_quarter] = total
+            sketch2(j).start()
+
+    def sketches_across():
+        wait(part.at[pl.ds(48, 15)], brecv.at[1])
+        part[pl.ds(64 + 4 * t, 4)] = part[pl.ds(48 + 4 * x, 4)]
+        for m in range(7, 0, -1):
+            sketch3(m).start()
 
     def moments_back():
         wait(part.at[pl.ds(16, 15)], mrecv.at[1])
@@ -409,18 +391,26 @@
 
     def invert(matrices):
         eye = jnp.where(rem(lane64, HALF) == row64, 1.0, 0.0).astype(F32)
-        first, gains = chebyshev()
-        state = [(eye - first * a, first * eye) for a in matrices]
-        for g in gains:
-            following = []
+        weight, start = chebyshev()
+
+        def double(_, carry):
+            value, state = carry
+            following = 2.0 * value * value - 1.0
+            g = 2.0 * value * value / following
+            doubled = []
             for left_over, inverse in state:
                 both = product(
                     jnp.concatenate([left_over, inverse], axis=0), wide(left_over)
                 )
-                following.append(
+                doubled.append(
                     (g * both[:HALF] - (g - 1.0) * eye, g * (inverse + both[HALF:]))
                 )
-            state = following
+            return following, tuple(doubled)
+
+        state = tuple((eye - weight * a, weight * eye) for a in matrices)
+        _, state = lax.fori_loop(
+            0, DOUBLINGS, double, (jnp.full((1, BLOCK), start, F32), state)
+        )
         results = []
         for a, (_, inverse) in zip(matrices, state):
             error = exact(a, wide(inverse))
@@ -449,57 +439,51 @@
         return inv_out * (live / trace_out), inv_in * (live / trace_in)
 
     def diagonal_or_not(f):
-        pl.when(on_diagonal)(functools.partial(f, 15))
-        unless(on_diagonal)(functools.partial(f, 16))
+        pl.when(on_diagonal)(functools.partial(f, 31))
+        unless(on_diagonal)(functools.partial(f, 32))
 
     def solve(inv_out, inv_in):
         with scope("wait_sketches"):
-            diagonal_or_not(lambda n: wait(part.at[pl.ds(48, n)], brecv.at[1]))
+            wait(part.at[pl.ds(64, 28)], brecv.at[2])
         wide_out = wide(inv_out)
         solved = []
-        for e in range(4):
-            sketch = part[48 + 4 * e : 52 + 4 * e].reshape(HALF, BLOCK)
+        for e in range(8):
+            sketch = jnp.concatenate(
+                [part[64 + 4 * (4 * (e % 2) + q) + e // 2] for q in range(4)], axis=0
+            )
             solved.append(
                 fold(product(wide_out, jnp.concatenate([sketch, sketch], axis=0)))
             )
         return product(jnp.concatenate(solved, axis=0), wide(inv_in))
 
     def final(a, tt):
-        return remote(msg.at[a], fin.at[d], fsend, frecv, 2 * t + a, tt)
+        return remote(msg.at[a], fin.at[d * 2 + z], fsend, frecv, 4 * x + a, tt)
 
     def score(weights, scale):
         with scope("wait_share"):
             for r in range(2):
-                wait(qall.at[pl.ds(r * 8, 7)], qrecv.at[r])
+                wait(qall.at[pl.ds(0, 3)], qrecv.at[r])
         queries = qall[...]
         rows = []
-        for e in range(4):
+        for e in range(8):
             rows.append(
                 jnp.sum(queries * weights[e * HALF : (e + 1) * HALF][None], axis=1)
             )
-        rows = jnp.concatenate(rows, axis=0)
-        ones = jnp.ones((16, BLOCK), F32)
-        sums = lax.dot_general(
-            ones, rows, (((1,), (1,)), ((), ())),
-            precision=lax.Precision.HIGHEST, preferred_element_type=F32,
-        )
-        row = lax.broadcasted_iota(jnp.int32, (16, HALF), 0)
-        lane = lax.broadcasted_iota(jnp.int32, (16, HALF), 1)
-        example = div(lane, 16)
-        kept = jnp.logical_and(
-            rem(row, 8) < 2, example == 2 * div(row, 8) + rem(row, 8)
-        )
-        sums = jnp.where(kept, sums * scale, 0.0)
-        at_row = lax.broadcasted_iota(jnp.int32, (HALF, BLOCK), 0)
-        at_lane = lax.broadcasted_iota(jnp.int32, (HALF, BLOCK), 1)
-        query = 2 * rem(at_row, 8) + rem(div(at_row, 8), 2)
-        place = jnp.where(at_lane == rem(d, 8) * 16 + query, 1.0, 0.0).astype(F32)
-        msg[...] = exact(sums, place).reshape(2, 8, BLOCK)
-
-        @pl.loop(0, 16)
+        sums = exact(jnp.concatenate(rows, axis=0), jnp.ones((BLOCK, BLOCK), F32))
+        row = lax.broadcasted_iota(jnp.int32, (HALF, BLOCK), 0)
+        lane = lax.broadcasted_iota(jnp.int32, (HALF, BLOCK), 1)
+        query = 8 * z + 2 * rem(row, 4) + rem(div(row, 4), 2)
+        sums = jnp.where(lane == rem(d, 8) * 16 + query, sums * scale, 0.0)
+        sums = [
+            jnp.sum(sums[e * 8 : (e + 1) * 8], axis=0, keepdims=True) for e in range(8)
+        ]
+        for a in range(4):
+            msg[a] = jnp.concatenate(sums[2 * a : 2 * a + 2], axis=0)
+
+        @pl.loop(0, 32)
         def _(j):
             a, tt = div(j, 8), rem(j, 8)
-            me = is_me(2 * t + a, tt)
+            me = is_me(4 * x + a, tt)
 
             @unless(me)
             def _():
@@ -507,29 +491,45 @@
 
             @pl.when(me)
             def _():
-                fin[d] = msg[a]
+                fin[d * 2 + z] = msg[a]
 
     def do(name, f, *args):
         with scope(name):
             return f(*args)
 
-    do("project_0", project_pairs, 0, 4)
-    do("project_1", project_pairs, 4, 8)
-    do("halve2_0", halve2, 0)
-    do("halve1_1", halve1, 1)
-    do("project_2a", project_pairs, 8, 11)
-    do("halve3_0", halve3, 0)
-    do("project_2b", project_pairs, 11, 12)
+    @pl.loop(0, 6)
+    def _(four):
+        do("project", project, four)
+
+        @pl.when(four == 0)
+        def _():
+            do("barrier_wait", everyone_is_here)
+            send_items((2, 7), (1, 7), (0, 6), (2, 6), (1, 6), (0, 5), (2, 5), (2, 4))
+
+        @pl.when(four == 1)
+        def _():
+            send_items((1, 3), (0, 2), (1, 2), (0, 1))
+
+        @pl.when(four == 3)
+        def _():
+            do("halve2_0", halve2, 0)
+            do("halve1_1", halve1, 1)
+
+        @pl.when(four == 4)
+        def _():
+            do("halve3_0", halve3, 0)
+
+    do("halve1_2", halve1, 2)
+    do("halve2_1", halve2, 1)
     do("train_finish", train_finish)
-    do("halve2_1", halve2, 1)
-    do("halve1_2", halve1, 2)
-    do("moments_over_dp", moments_over_dp)
     do("halve3_1", halve3, 1)
     do("halve2_2", halve2, 2)
+    do("moments_over_dp", moments_over_dp)
     do("sketches_out", sketches_out)
     do("share_1", share_sketch, 1)
+    do("halve3_2", halve3, 2)
     do("moments_back", moments_back)
-    do("halve3_2", halve3, 2)
+    do("sketches_across", sketches_across)
     do("share_2", share_sketch, 2)
     inv_out, inv_in = do("inverses", inverses)
     weights = do("solve", solve, inv_out, inv_in)
@@ -540,18 +540,18 @@
     with scope("drain"):
         wait(acc.at[pl.ds(0, 21)], send)
         wait(part.at[pl.ds(0, 29)], msend)
-        diagonal_or_not(lambda n: wait(part.at[pl.ds(0, n + 3)], bsend))
-        wait(qall.at[pl.ds(0, 14)], qsend)
+        wait(part.at[pl.ds(0, 46)], bsend)
+        wait(qall.at[pl.ds(0, 6)], qsend)
     with scope("final_wait"):
         diagonal_or_not(lambda n: wait(fin.at[pl.ds(0, n)], frecv))
     with scope("final_drain"):
         diagonal_or_not(lambda n: wait(fin.at[pl.ds(0, n)], fsend))
-    low, high = fin[0], fin[8]
-    for j in range(1, 8):
+    low, high = fin[0], fin[16]
+    for j in range(1, 16):
         low = low + fin[j]
-        high = high + fin[j + 8]
-    out_ref[:, :BLOCK] = low[:2]
-    out_ref[:, BLOCK:] = high[:2]
+        high = high + fin[j + 16]
+    out_ref[:, :BLOCK] = low
+    out_ref[:, BLOCK:] = high
 
 
 def on_device(tin, tgr, tlen, qin, qgr, qlen, pin, pout):
@@ -567,21 +567,21 @@
             pltpu.SMEM(tlen.shape, jnp.int32),
             pltpu.SMEM(qlen.shape, jnp.int32),
             pltpu.VMEM((12, 2 * BLOCK, features), BF16),
-            pltpu.VMEM((12, 2, 2 * BLOCK, units), BF16),
+            pltpu.VMEM((2, 24 * BLOCK, units), BF16),
             pltpu.VMEM((2, BLOCK, features), BF16),
             pltpu.VMEM((2, BLOCK, units), BF16),
             pltpu.VMEM((24, HALF + BLOCK, BLOCK), F32),
             pltpu.VMEM((24, HALF + BLOCK, BLOCK), F32),
             pltpu.VMEM((3, 3, 2, HALF, BLOCK), F32),
             pltpu.VMEM((3, 3, HALF, BLOCK), F32),
-            pltpu.VMEM((64, 16, BLOCK), F32),
+            pltpu.VMEM((96, 16, BLOCK), F32),
             pltpu.VMEM((16, BLOCK), F32),
             pltpu.VMEM((16, BLOCK), F32),
-            pltpu.VMEM((16, HALF, BLOCK), F32),
-            pltpu.VMEM((2, 8, BLOCK), F32),
-            pltpu.VMEM((16, 8, BLOCK), F32),
+            pltpu.VMEM((8, HALF, BLOCK), F32),
+            pltpu.VMEM((4, 2, BLOCK), F32),
+            pltpu.VMEM((32, 2, BLOCK), F32),
             dma((4,)), dma((4,)), dma((4,)),
-            dma, dma((3, 3)), dma((3, 3)), dma((3, 3)), dma, dma((3,)), dma, dma((2,)), dma, dma((2,)), dma, dma,
+            dma, dma((3, 3)), dma((2, 3)), dma((2, 3)), dma, dma((3,)), dma, dma((3,)), dma, dma((2,)), dma, dma,
         ],
         compiler_params=pltpu.CompilerParams(
             collective_id=0, has_side_effects=True, vmem_limit_bytes=56 * 1024 * 1024

time: 57.9 us -> 48.7 us (0.84)
  Pallas kernels: 56.5 us -> 47.3 us
    pallas_call x1, Pallas kernels: 56.5 us -> 47.3 us  [on_device(): pl.pallas_call(kernel, out_shape=jax.ShapeDtypeStruct((tin.shape[0], DP *...]
where the time goes in v3:
time: 48.7 us; the launch traced here: 48.6 us
  Pallas kernels  47.3 us (97%)
  local copies, waits for them, and re-layouts  1.26 us (3%)
    pallas_call x1, Pallas kernels, on_device(): pl.pallas_call(kernel, out_shape=jax.ShapeDtypeStruct((tin.shape[0], DP *...  47.3 us
    unnamed x1, local copies, waits for them, and re-layouts  1.26 us

profile of v3, /device:TPU:1, one launch (start us, length us, event | category | flops | bytes accessed | tf_op | source)
XLA Modules:
  0.0 48.6 jit_solution(2853753059827065447)
XLA Ops:
  0.0 47.3 %shard_map.82 = f32[2,256]{1,0:T(2,128)} custom-call(s32[2]{0:T(128)} %tlen_hbm.1, s32[16]{0:T(128)} %qlen_hbm.1, bf16[2,512,512]{2,1,0:T(8,128)(2,1)} %tin.1, bf16[2,2,512,1792]{3,2,1,0:T(8,128)(2,1)} %tgr.1, bf16[16,128,512]{2,1,0:T(8,128)(2,1)} %qin.1, bf16[16,2,128,1792]{3,2,1,0:T(8,128)(2,1)} %qgr.1, bf16[64,512]{1,0:T(8,128)(2,1)} %bitcast.3, ...), custom_call_target="tpu_custom_call" | custom-call | tf_op jit(solution)/shard_map/pallas_call | solution.py:561
  47.3 1.3 %copy.10 = f32[2,256]{1,0:T(2,128)} copy(f32[2,256]{1,0:T(2,128)} %shard_map.82) | data formatting | bytes 4096

commit v4 on v3

--- a/solution.py
+++ b/solution.py
@@ -121,21 +121,13 @@
 
     with scope("greet"):
 
-        @pl.loop(1, 8)
-        def _(m):
-            greet(d, flip(m))
-
         @pl.loop(1, 16)
         def _(j):
             greet(rem(d + j, DP), t)
 
-        @pl.loop(0, 32)
-        def _(j):
-            dd, tt = div(j, 2), rem(j, 2) * 4 + column
-
-            @unless(is_me(dd, tt))
-            def _():
-                greet(dd, tt)
+        @pl.loop(1, 8)
+        def _(m):
+            greet(d, flip(8 - m))
 
     with scope("weights"):
         wip[0, RANK:] = jnp.zeros(pin.shape, BF16)
@@ -199,8 +191,7 @@
             first(0, p, m, m ^ GENS[p][0]).start()
 
     def everyone_is_here():
-        pl.when(on_diagonal)(lambda: pl.semaphore_wait(barrier, 53))
-        unless(on_diagonal)(lambda: pl.semaphore_wait(barrier, 54))
+        pl.semaphore_wait(barrier, 22)
 
     def halve1(r):
         for k in range(4):

time: 48.7 us -> 47.3 us (0.971)
  Pallas kernels: 47.3 us -> 45.9 us
    pallas_call x1, Pallas kernels: 47.3 us -> 45.9 us  [on_device(): pl.pallas_call(kernel, out_shape=jax.ShapeDtypeStruct((tin.shape[0], DP *...]
where the time goes in v4:
time: 47.3 us; the launch traced here: 47.2 us
  Pallas kernels  45.9 us (97%)
  local copies, waits for them, and re-layouts  1.26 us (3%)
    pallas_call x1, Pallas kernels, on_device(): pl.pallas_call(kernel, out_shape=jax.ShapeDtypeStruct((tin.shape[0], DP *...  45.9 us
    unnamed x1, local copies, waits for them, and re-layouts  1.26 us

profile of v4, /device:TPU:1, one launch (start us, length us, event | category | flops | bytes accessed | tf_op | source)
XLA Modules:
  0.0 47.2 jit_solution(14497254156063532718)
XLA Ops:
  0.0 45.9 %shard_map.82 = f32[2,256]{1,0:T(2,128)} custom-call(s32[2]{0:T(128)} %tlen_hbm.1, s32[16]{0:T(128)} %qlen_hbm.1, bf16[2,512,512]{2,1,0:T(8,128)(2,1)} %tin.1, bf16[2,2,512,1792]{3,2,1,0:T(8,128)(2,1)} %tgr.1, bf16[16,128,512]{2,1,0:T(8,128)(2,1)} %qin.1, bf16[16,2,128,1792]{3,2,1,0:T(8,128)(2,1)} %qgr.1, bf16[64,512]{1,0:T(8,128)(2,1)} %bitcast.3, ...), custom_call_target="tpu_custom_call" | custom-call | tf_op jit(solution)/shard_map/pallas_call | solution.py:552
  45.9 1.3 %copy.10 = f32[2,256]{1,0:T(2,128)} copy(f32[2,256]{1,0:T(2,128)} %shard_map.82) | data formatting | bytes 4096

commit v5 on v4

--- a/solution.py
+++ b/solution.py
@@ -25,7 +25,7 @@
 HALF = 64
 DP = 16
 DOUBLINGS = 7
-GENS = ((1, 3, 4), (3, 4, 1), (4, 1, 3))
+ROUTES = ((1, 5, 4, 1), (3, 2, 1, 2), (4, 7, 3, 0))
 
 
 def chebyshev():
@@ -49,8 +49,8 @@
 
 def kernel(
     tlen_hbm, qlen_hbm, tin, tgr, qin, qgr, pin, pout, out_ref,
-    tlen, qlen, xin, xgr, wip, wop, acc, got, got2, got3, part, msum, bsum, qall, msg, fin,
-    wsem, isem, gsem, send, recv1, recv2, recv3, msend, mrecv, bsend, brecv, qsend, qrecv, fsend, frecv,
+    tlen, qlen, xin, xgr, wip, wop, acc, far, near, last, part, msum, bsum, qall, msg, fin,
+    wsem, isem, gsem, send, recv1, recv2, msend, mrecv, bsend, brecv, qsend, qrecv, fsend, frecv,
 ):
     d = lax.axis_index("dp").astype(jnp.int32)
     t = lax.axis_index("tensor").astype(jnp.int32)
@@ -80,21 +80,23 @@
     def unless(condition):
         return pl.when(jnp.logical_not(condition))
 
-    def load(pair, query):
-        sem = rem(pair, 4)
-        m = 7 - 2 * sem
-        for h in range(2):
-            item = flip(m - h)
+    def items(four):
+        second = rem(four, 2)
+        return (7 - 3 * second, 6 - 3 * second, 5 - 4 * second, 2 - 2 * second)
+
+    def load(four, query):
+        sem = rem(four, 2)
+        for k, m in enumerate(items(four)):
+            item = flip(m)
             if query:
-                q = item * 2 + (div(pair, 4) - 1)
+                q = item * 2 + (div(four, 2) - 1)
                 a, b = qin.at[q], qgr.at[q]
             else:
                 rows = pl.ds(pl.multiple_of(rem(item, 4) * BLOCK, BLOCK), BLOCK)
                 e = div(item, 4)
                 a, b = tin.at[e, rows, :], tgr.at[e, :, rows, :]
-            to = pl.ds(h * BLOCK, BLOCK)
-            pltpu.make_async_copy(a, xin.at[pair, to], isem.at[sem]).start()
-            to = pl.ds((pair * 2 + h) * BLOCK, BLOCK)
+            to = pl.ds((four * 4 + k) * BLOCK, BLOCK)
+            pltpu.make_async_copy(a, xin.at[to], isem.at[sem]).start()
             pltpu.make_async_copy(b, xgr.at[:, to], gsem.at[sem]).start()
 
     with scope("start_loads"):
@@ -103,9 +105,9 @@
         pltpu.make_async_copy(pout.at[0], wop.at[0, :RANK], wsem.at[1]).start()
         pltpu.make_async_copy(pout.at[1], wop.at[1, RANK:], wsem.at[1]).start()
 
-        @pl.loop(0, 4)
-        def _(pair):
-            load(pair, False)
+        @pl.loop(0, 2)
+        def _(four):
+            load(four, False)
 
         lengths = (
             pltpu.make_async_copy(tlen_hbm, tlen, wsem.at[2]),
@@ -139,97 +141,59 @@
         for c in lengths:
             c.wait()
 
-    def rows_of(p):
-        return slice(HALF * p, HALF * (p + 1))
-
-    def piece(r, p, m):
-        return acc.at[r * 8 + m, rows_of(p)]
-
-    def first(r, p, m, s):
-        return remote(
-            piece(r, p, m), got.at[r * 8 + s, rows_of(p)],
-            send, recv1.at[r, p], d, flip(GENS[p][0]),
-        )
-
     def times(rows, turned):
         return lax.dot_general(
             rows, turned, (((1,), (1,)), ((), ())), preferred_element_type=F32
         )
 
     def project(four):
-        pairs = (2 * four, 2 * four + 1)
-        for pair in pairs:
-            sem = rem(pair, 4)
-            wait(xin.at[pair], isem.at[sem])
-            wait(xgr.at[:, pl.ds(pair * 2 * BLOCK, 2 * BLOCK)], gsem.at[sem])
+        r, sem = div(four, 2), rem(four, 2)
+        rows = pl.ds(four * 4 * BLOCK, 4 * BLOCK)
+        wait(xin.at[rows], isem.at[sem])
+        wait(xgr.at[:, rows], gsem.at[sem])
 
         @pl.when(four < 4)
         def _():
-            for pair in pairs:
-                load(pair + 4, True)
-
-        def rows(start):
-            return jnp.concatenate(
-                [
-                    xin[pair, h * BLOCK + start : h * BLOCK + start + HALF]
-                    for pair in pairs
-                    for h in range(2)
-                ],
-                axis=0,
-            )
-
-        ins = times(rows(0), wip[0]) + times(rows(HALF), wip[1])
-        units = pl.ds(four * 4 * BLOCK, 4 * BLOCK)
-        outs = times(xgr[0, units], wop[0]) + times(xgr[1, units], wop[1])
-        for i in range(4):
-            slot = div(four, 2) * 8 + 7 - 4 * rem(four, 2) - i
-            acc[slot, :HALF] = ins[i * HALF : (i + 1) * HALF]
-            acc[slot, HALF:] = outs[i * BLOCK : (i + 1) * BLOCK]
-
-    def send_items(*which):
-        for p, m in which:
-            first(0, p, m, m ^ GENS[p][0]).start()
+            load(four + 2, True)
+
+        ins = xin[rows].reshape(4, 2, HALF, -1)
+        ins = times(ins[:, 0].reshape(4 * HALF, -1), wip[0]) + times(
+            ins[:, 1].reshape(4 * HALF, -1), wip[1]
+        )
+        outs = times(xgr[0, rows], wop[0]) + times(xgr[1, rows], wop[1])
+        for k, m in enumerate(items(four)):
+            slot = r * 8 + m
+            acc[slot, :HALF] = ins[k * HALF : (k + 1) * HALF]
+            acc[slot, HALF:] = outs[k * BLOCK : (k + 1) * BLOCK]
 
     def everyone_is_here():
         pl.semaphore_wait(barrier, 22)
 
-    def halve1(r):
-        for k in range(4):
-            for p, (g1, g2, g3) in enumerate(GENS):
-                s = (g2, g2 ^ g3, g3, 0)[k]
-                first(r, p, s ^ g1, s).start()
-
-    def add(r, p, s, ref):
-        rows = rows_of(p)
-        acc[r * 8 + s, rows] = acc[r * 8 + s, rows] + ref[...]
-
-    def halve2(r):
-        for p, (_, g2, g3) in enumerate(GENS):
-            wait(qall.at[pl.ds(0, 4)], recv1.at[r, p])
-            for k, s in enumerate((g2, g2 ^ g3)):
-                add(r, p, s, got.at[r * 8 + s, rows_of(p)])
-                remote(
-                    piece(r, p, s), got2.at[r, p, k],
-                    send, recv2.at[r % 2, p], d, flip(g2),
-                ).start()
-        for p, (_, _, g3) in enumerate(GENS):
-            for s in (g3, 0):
-                add(r, p, s, got.at[r * 8 + s, rows_of(p)])
-
-    def halve3(r):
-        for p, (_, _, g3) in enumerate(GENS):
-            wait(qall.at[pl.ds(0, 2)], recv2.at[r % 2, p])
-            add(r, p, g3, got2.at[r, p, 1])
+    def phase1(r):
+        for k, (g, _, _, p) in enumerate(ROUTES):
             remote(
-                piece(r, p, g3), got3.at[r, p], send, recv3.at[r % 2, p], d, flip(g3)
+                acc.at[r * 8 + 6, pl.ds(HALF * p, HALF)], far.at[r, k],
+                send, recv1.at[r, k], d, flip(6 ^ g),
             ).start()
-        for p in range(3):
-            add(r, p, 0, got2.at[r, p, 0])
-
-    def halved(r):
-        for p in range(3):
-            wait(qall.at[0], recv3.at[r % 2, p])
-        return acc[r * 8] + jnp.concatenate([got3[r, p] for p in range(3)], axis=0)
+        for k, (_, item, via, _) in enumerate(ROUTES):
+            remote(
+                acc.at[r * 8 + item], near.at[r, k], send, recv1.at[r, k], d, flip(via)
+            ).start()
+
+    def phase2(r):
+        for k, (g, _, _, p) in enumerate(ROUTES):
+            wait(part.at[pl.ds(0, 16)], recv1.at[r, k])
+            mine = r * 8 + g
+            rows = slice(HALF * p, HALF * (p + 1))
+            acc[mine] = acc[mine] + near[r, k]
+            acc[mine, rows] = acc[mine, rows] + far[r, k]
+            remote(
+                acc.at[mine], last.at[r, k], send, recv2.at[r], d, flip(g)
+            ).start()
+
+    def summed(r):
+        wait(last.at[r], recv2.at[r])
+        return acc[r * 8] + last[r, 0] + last[r, 1] + last[r, 2]
 
     row64 = lax.broadcasted_iota(jnp.int32, (HALF, BLOCK), 0)
     lane64 = lax.broadcasted_iota(jnp.int32, (HALF, BLOCK), 1)
@@ -264,8 +228,8 @@
         return remote(mine, mine, qsend, qrecv.at[r - 1], d, flip(m))
 
     def share_sketch(r):
-        with scope("halved"):
-            total = halved(r)
+        with scope("summed"):
+            total = summed(r)
         qall[(r - 1) * 4 + x] = query_sketch(total, r)
         for m in (2, 1, 3):
             share(r, m).start()
@@ -296,8 +260,8 @@
         )
 
     def train_finish():
-        with scope("halved"):
-            total = halved(0)
+        with scope("summed"):
+            total = summed(0)
         length = tlen[z] - x * BLOCK
         twice, outputs, turned = finished(total, length)
         products = jnp.dot(
@@ -495,30 +459,26 @@
         @pl.when(four == 0)
         def _():
             do("barrier_wait", everyone_is_here)
-            send_items((2, 7), (1, 7), (0, 6), (2, 6), (1, 6), (0, 5), (2, 5), (2, 4))
-
-        @pl.when(four == 1)
+            phase1(0)
+
+        @pl.when(four == 2)
         def _():
-            send_items((1, 3), (0, 2), (1, 2), (0, 1))
+            phase1(1)
 
         @pl.when(four == 3)
         def _():
-            do("halve2_0", halve2, 0)
-            do("halve1_1", halve1, 1)
+            do("phase2_0", phase2, 0)
 
         @pl.when(four == 4)
         def _():
-            do("halve3_0", halve3, 0)
-
-    do("halve1_2", halve1, 2)
-    do("halve2_1", halve2, 1)
+            phase1(2)
+
     do("train_finish", train_finish)
-    do("halve3_1", halve3, 1)
-    do("halve2_2", halve2, 2)
+    do("phase2_1", phase2, 1)
     do("moments_over_dp", moments_over_dp)
+    do("phase2_2", phase2, 2)
     do("sketches_out", sketches_out)
     do("share_1", share_sketch, 1)
-    do("halve3_2", halve3, 2)
     do("moments_back", moments_back)
     do("sketches_across", sketches_across)
     do("share_2", share_sketch, 2)
@@ -557,22 +517,22 @@
         scratch_shapes=[
             pltpu.SMEM(tlen.shape, jnp.int32),
             pltpu.SMEM(qlen.shape, jnp.int32),
-            pltpu.VMEM((12, 2 * BLOCK, features), BF16),
+            pltpu.VMEM((24 * BLOCK, features), BF16),
             pltpu.VMEM((2, 24 * BLOCK, units), BF16),
             pltpu.VMEM((2, BLOCK, features), BF16),
             pltpu.VMEM((2, BLOCK, units), BF16),
             pltpu.VMEM((24, HALF + BLOCK, BLOCK), F32),
-            pltpu.VMEM((24, HALF + BLOCK, BLOCK), F32),
-            pltpu.VMEM((3, 3, 2, HALF, BLOCK), F32),
             pltpu.VMEM((3, 3, HALF, BLOCK), F32),
+            pltpu.VMEM((3, 3, HALF + BLOCK, BLOCK), F32),
+            pltpu.VMEM((3, 3, HALF + BLOCK, BLOCK), F32),
             pltpu.VMEM((96, 16, BLOCK), F32),
             pltpu.VMEM((16, BLOCK), F32),
             pltpu.VMEM((16, BLOCK), F32),
             pltpu.VMEM((8, HALF, BLOCK), F32),
             pltpu.VMEM((4, 2, BLOCK), F32),
             pltpu.VMEM((32, 2, BLOCK), F32),
-            dma((4,)), dma((4,)), dma((4,)),
-            dma, dma((3, 3)), dma((2, 3)), dma((2, 3)), dma, dma((3,)), dma, dma((3,)), dma, dma((2,)), dma, dma,
+            dma((4,)), dma((2,)), dma((2,)),
+            dma, dma((3, 3)), dma((3,)), dma, dma((3,)), dma, dma((3,)), dma, dma((2,)), dma, dma,
         ],
         compiler_params=pltpu.CompilerParams(
             collective_id=0, has_side_effects=True, vmem_limit_bytes=56 * 1024 * 1024

time: 47.3 us -> 45.9 us (0.970)
  Pallas kernels: 45.9 us -> 44.5 us
    pallas_call x1, Pallas kernels: 45.9 us -> 44.5 us  [on_device(): pl.pallas_call(kernel, out_shape=jax.ShapeDtypeStruct((tin.shape[0], DP *...]
where the time goes in v5:
time: 45.9 us; the launch traced here: 45.8 us
  Pallas kernels  44.5 us (97%)
  local copies, waits for them, and re-layouts  1.26 us (3%)
    pallas_call x1, Pallas kernels, on_device(): pl.pallas_call(kernel, out_shape=jax.ShapeDtypeStruct((tin.shape[0], DP *...  44.5 us
    unnamed x1, local copies, waits for them, and re-layouts  1.26 us

profile of v5, /device:TPU:1, one launch (start us, length us, event | category | flops | bytes accessed | tf_op | source)
XLA Modules:
  0.0 45.8 jit_solution(232548798604101734)
XLA Ops:
  0.0 44.5 %shard_map.82 = f32[2,256]{1,0:T(2,128)} custom-call(s32[2]{0:T(128)} %tlen_hbm.1, s32[16]{0:T(128)} %qlen_hbm.1, bf16[2,512,512]{2,1,0:T(8,128)(2,1)} %tin.1, bf16[2,2,512,1792]{3,2,1,0:T(8,128)(2,1)} %tgr.1, bf16[16,128,512]{2,1,0:T(8,128)(2,1)} %qin.1, bf16[16,2,128,1792]{3,2,1,0:T(8,128)(2,1)} %qgr.1, bf16[64,512]{1,0:T(8,128)(2,1)} %bitcast.3, ...), custom_call_target="tpu_custom_call" | custom-call | tf_op jit(solution)/shard_map/pallas_call | solution.py:512
  44.5 1.3 %copy.10 = f32[2,256]{1,0:T(2,128)} copy(f32[2,256]{1,0:T(2,128)} %shard_map.82) | data formatting | bytes 4096

commit v6 on v5

--- a/solution.py
+++ b/solution.py
@@ -57,6 +57,8 @@
     z, x = div(t, 4), rem(t, 4)
     column = div(d, 4)
     on_diagonal = column == x
+    core, chip = rem(d, 2), div(d, 2)
+    leads = core == 1
 
     def flip(m):
         m = jnp.int32(m)
@@ -235,15 +237,18 @@
             share(r, m).start()
 
     def moment1(m):
-        return remote(part.at[flip(m)], part.at[8 + m], msend, mrecv.at[0], d, flip(m))
+        slot = 16 - 8 * core + m
+        return remote(
+            part.at[flip(m)], part.at[slot], msend, mrecv.at[0], 2 * chip + 1, flip(m)
+        )
 
     def moment2(j):
-        return remote(msum, part.at[16 + d], msend, mrecv.at[1], rem(d + j, DP), t)
-
-    def moment3(m):
-        return remote(
-            part.at[32 + t], part.at[32 + t], msend, mrecv.at[2], d, flip(m)
-        )
+        other = 2 * rem(chip + j, 8) + 1
+        return remote(msum, part.at[24 + chip], msend, mrecv.at[1], other, t)
+
+    def moment3(m, to):
+        piece = part.at[32 + t]
+        return remote(piece, piece, msend, mrecv.at[2], 2 * chip + to, flip(m))
 
     def sketch1(m):
         return remote(
@@ -275,21 +280,22 @@
         part[4:8] = jnp.where(left, ins[:HALF], live).reshape(4, 16, BLOCK)
         for m in range(7, 0, -1):
             moment1(m).start()
+        unless(leads)(lambda: moment1(0).start())
         part[40:44] = fold(products[:, BLOCK:]).reshape(4, 16, BLOCK)
         for m in range(1, 4):
             sketch1(m).start()
 
     def moments_over_dp():
-        wait(part.at[pl.ds(9, 7)], mrecv.at[0])
-        total = part[t]
-        for m in range(1, 8):
-            total = total + part[8 + m]
-        msum[...] = total
-        part[16 + d] = total
-
-        @pl.loop(1, 16)
-        def _(j):
-            moment2(j).start()
+        @pl.when(leads)
+        def _():
+            wait(part.at[pl.ds(9, 15)], mrecv.at[0])
+            total = part[t]
+            for slot in range(9, 24):
+                total = total + part[slot]
+            msum[...] = total
+            part[24 + chip] = total
+            for j in range(1, 8):
+                moment2(j).start()
 
     def sketches_out():
         wait(part.at[pl.ds(45, 3)], brecv.at[0])
@@ -310,13 +316,17 @@
             sketch3(m).start()
 
     def moments_back():
-        wait(part.at[pl.ds(16, 15)], mrecv.at[1])
-        total = part[16]
-        for j in range(1, 16):
-            total = total + part[16 + j]
-        part[32 + t] = total
-        for m in range(7, 0, -1):
-            moment3(m).start()
+        @pl.when(leads)
+        def _():
+            wait(part.at[pl.ds(24, 7)], mrecv.at[1])
+            total = part[24]
+            for slot in range(25, 32):
+                total = total + part[slot]
+            part[32 + t] = total
+            for m in range(7, -1, -1):
+                moment3(m, 0).start()
+                if m:
+                    moment3(m, 1).start()
 
     def wide(v):
         zero = jnp.zeros_like(v)
@@ -374,7 +384,8 @@
 
     def inverses():
         with scope("wait_moment3"):
-            wait(part.at[pl.ds(32, 7)], mrecv.at[2])
+            pl.when(leads)(lambda: wait(part.at[pl.ds(32, 7)], mrecv.at[2]))
+            unless(leads)(lambda: wait(part.at[pl.ds(32, 8)], mrecv.at[2]))
         whole = part[32:40].reshape(2 * HALF, BLOCK)
         outs, ins = whole[:HALF], whole[HALF:]
         live = jnp.max(jnp.where(left, 0.0, ins))
@@ -475,9 +486,9 @@
 
     do("train_finish", train_finish)
     do("phase2_1", phase2, 1)
+    do("sketches_out", sketches_out)
     do("moments_over_dp", moments_over_dp)
     do("phase2_2", phase2, 2)
-    do("sketches_out", sketches_out)
     do("share_1", share_sketch, 1)
     do("moments_back", moments_back)
     do("sketches_across", sketches_across)
@@ -490,7 +501,8 @@
 
     with scope("drain"):
         wait(acc.at[pl.ds(0, 21)], send)
-        wait(part.at[pl.ds(0, 29)], msend)
+        pl.when(leads)(lambda: wait(part.at[pl.ds(0, 29)], msend))
+        unless(leads)(lambda: wait(part.at[pl.ds(0, 8)], msend))
         wait(part.at[pl.ds(0, 46)], bsend)
         wait(qall.at[pl.ds(0, 6)], qsend)
     with scope("final_wait"):

time: 45.9 us -> 45 us (0.980)
  Pallas kernels: 44.5 us -> 43.6 us
    pallas_call x1, Pallas kernels: 44.5 us -> 43.6 us  [on_device(): pl.pallas_call(kernel, out_shape=jax.ShapeDtypeStruct((tin.shape[0], DP *...]
where the time goes in v6:
time: 45 us; the launch traced here: 44.9 us
  Pallas kernels  43.6 us (97%)
  local copies, waits for them, and re-layouts  1.26 us (3%)
    pallas_call x1, Pallas kernels, on_device(): pl.pallas_call(kernel, out_shape=jax.ShapeDtypeStruct((tin.shape[0], DP *...  43.6 us
    unnamed x1, local copies, waits for them, and re-layouts  1.26 us

profile of v6, /device:TPU:1, one launch (start us, length us, event | category | flops | bytes accessed | tf_op | source)
XLA Modules:
  0.0 44.9 jit_solution(7083399694976336892)
XLA Ops:
  0.0 43.6 %shard_map.82 = f32[2,256]{1,0:T(2,128)} custom-call(s32[2]{0:T(128)} %tlen_hbm.1, s32[16]{0:T(128)} %qlen_hbm.1, bf16[2,512,512]{2,1,0:T(8,128)(2,1)} %tin.1, bf16[2,2,512,1792]{3,2,1,0:T(8,128)(2,1)} %tgr.1, bf16[16,128,512]{2,1,0:T(8,128)(2,1)} %qin.1, bf16[16,2,128,1792]{3,2,1,0:T(8,128)(2,1)} %qgr.1, bf16[64,512]{1,0:T(8,128)(2,1)} %bitcast.3, ...), custom_call_target="tpu_custom_call" | custom-call | tf_op jit(solution)/shard_map/pallas_call | solution.py:524
  43.6 1.3 %copy.10 = f32[2,256]{1,0:T(2,128)} copy(f32[2,256]{1,0:T(2,128)} %shard_map.82) | data formatting | bytes 4096

commit v7 on v6

--- a/solution.py
+++ b/solution.py
@@ -256,13 +256,21 @@
         )
 
     def sketch2(j):
-        return remote(bsum, part.at[48 + d], bsend, brecv.at[1], rem(d + j, DP), t)
+        other = 2 * rem(chip + j, 8) + core
+        return remote(bsum, part.at[48 + chip], bsend, brecv.at[1], other, t)
+
+    scored = 64 + 16 * core
 
     def sketch3(m):
         return remote(
-            part.at[pl.ds(48 + 4 * rem(flip(m), 4), 4)], part.at[pl.ds(64 + 4 * t, 4)],
+            part.at[pl.ds(48 + 2 * rem(flip(m), 4), 2)],
+            part.at[pl.ds(scored + 2 * t, 2)],
             bsend, brecv.at[2], d, flip(m),
         )
+
+    def sketch4():
+        mine = part.at[pl.ds(scored, 16)]
+        return remote(mine, mine, bsend, brecv.at[3], 2 * chip + 1 - core, t)
 
     def train_finish():
         with scope("summed"):
@@ -303,17 +311,20 @@
         for m in range(1, 4):
             total = total + part[44 + m]
         bsum[...] = total
-        part[48 + d] = total
-
-        @pl.loop(1, 16)
-        def _(j):
+        part[48 + chip] = total
+        for j in range(1, 8):
             sketch2(j).start()
 
     def sketches_across():
-        wait(part.at[pl.ds(48, 15)], brecv.at[1])
-        part[pl.ds(64 + 4 * t, 4)] = part[pl.ds(48 + 4 * x, 4)]
+        wait(part.at[pl.ds(48, 7)], brecv.at[1])
+        part[pl.ds(scored + 2 * t, 2)] = part[pl.ds(48 + 2 * x, 2)]
         for m in range(7, 0, -1):
             sketch3(m).start()
+
+    def swap_sketches():
+        with scope("wait_sketches"):
+            wait(part.at[pl.ds(64, 14)], brecv.at[2])
+        sketch4().start()
 
     def moments_back():
         @pl.when(leads)
@@ -358,7 +369,8 @@
         eye = jnp.where(rem(lane64, HALF) == row64, 1.0, 0.0).astype(F32)
         weight, start = chebyshev()
 
-        def double(_, carry):
+        def double(i, carry):
+            pl.when(i == 5)(swap_sketches)
             value, state = carry
             following = 2.0 * value * value - 1.0
             g = 2.0 * value * value / following
@@ -409,14 +421,13 @@
         unless(on_diagonal)(functools.partial(f, 32))
 
     def solve(inv_out, inv_in):
-        with scope("wait_sketches"):
-            wait(part.at[pl.ds(64, 28)], brecv.at[2])
+        with scope("wait_swap"):
+            wait(part.at[pl.ds(64, 16)], brecv.at[3])
         wide_out = wide(inv_out)
         solved = []
         for e in range(8):
-            sketch = jnp.concatenate(
-                [part[64 + 4 * (4 * (e % 2) + q) + e // 2] for q in range(4)], axis=0
-            )
+            first = 64 + 16 * (e // 2 % 2) + 8 * (e % 2) + e // 4
+            sketch = jnp.concatenate([part[first + 2 * q] for q in range(4)], axis=0)
             solved.append(
                 fold(product(wide_out, jnp.concatenate([sketch, sketch], axis=0)))
             )
@@ -446,18 +457,18 @@
         for a in range(4):
             msg[a] = jnp.concatenate(sums[2 * a : 2 * a + 2], axis=0)
 
-        @pl.loop(0, 32)
+        @pl.loop(0, 8)
         def _(j):
-            a, tt = div(j, 8), rem(j, 8)
-            me = is_me(4 * x + a, tt)
-
-            @unless(me)
-            def _():
-                final(a, tt).start()
-
-            @pl.when(me)
-            def _():
-                fin[d * 2 + z] = msg[a]
+            tt = rem(t + 6 + j, 8)
+            for a in range(4):
+
+                @unless(is_me(4 * x + a, tt))
+                def _(a=a):
+                    final(a, tt).start()
+
+        @pl.when(on_diagonal)
+        def _():
+            fin[d * 2 + z] = msg[rem(d, 4)]
 
     def do(name, f, *args):
         with scope(name):
@@ -503,7 +514,7 @@
         wait(acc.at[pl.ds(0, 21)], send)
         pl.when(leads)(lambda: wait(part.at[pl.ds(0, 29)], msend))
         unless(leads)(lambda: wait(part.at[pl.ds(0, 8)], msend))
-        wait(part.at[pl.ds(0, 46)], bsend)
+        wait(part.at[pl.ds(0, 40)], bsend)
         wait(qall.at[pl.ds(0, 6)], qsend)
     with scope("final_wait"):
         diagonal_or_not(lambda n: wait(fin.at[pl.ds(0, n)], frecv))
@@ -544,7 +555,7 @@
             pltpu.VMEM((4, 2, BLOCK), F32),
             pltpu.VMEM((32, 2, BLOCK), F32),
             dma((4,)), dma((2,)), dma((2,)),
-            dma, dma((3, 3)), dma((3,)), dma, dma((3,)), dma, dma((3,)), dma, dma((2,)), dma, dma,
+            dma, dma((3, 3)), dma((3,)), dma, dma((3,)), dma, dma((4,)), dma, dma((2,)), dma, dma,
         ],
         compiler_params=pltpu.CompilerParams(
             collective_id=0, has_side_effects=True, vmem_limit_bytes=56 * 1024 * 1024

time: 45 us -> 44.4 us (0.987)
  Pallas kernels: 43.6 us -> 43 us
    pallas_call x1, Pallas kernels: 43.6 us -> 43 us  [on_device(): pl.pallas_call(kernel, out_shape=jax.ShapeDtypeStruct((tin.shape[0], DP *...]
where the time goes in v7:
time: 44.4 us; the launch traced here: 44.3 us
  Pallas kernels  43 us (97%)
  local copies, waits for them, and re-layouts  1.26 us (3%)
    pallas_call x1, Pallas kernels, on_device(): pl.pallas_call(kernel, out_shape=jax.ShapeDtypeStruct((tin.shape[0], DP *...  43 us
    unnamed x1, local copies, waits for them, and re-layouts  1.26 us

profile of v7, /device:TPU:1, one launch (start us, length us, event | category | flops | bytes accessed | tf_op | source)
XLA Modules:
  0.0 44.3 jit_solution(9137531093071752554)
XLA Ops:
  0.0 43.0 %shard_map.82 = f32[2,256]{1,0:T(2,128)} custom-call(s32[2]{0:T(128)} %tlen_hbm.1, s32[16]{0:T(128)} %qlen_hbm.1, bf16[2,512,512]{2,1,0:T(8,128)(2,1)} %tin.1, bf16[2,2,512,1792]{3,2,1,0:T(8,128)(2,1)} %tgr.1, bf16[16,128,512]{2,1,0:T(8,128)(2,1)} %qin.1, bf16[16,2,128,1792]{3,2,1,0:T(8,128)(2,1)} %qgr.1, bf16[64,512]{1,0:T(8,128)(2,1)} %bitcast.3, ...), custom_call_target="tpu_custom_call" | custom-call | tf_op jit(solution)/shard_map/pallas_call | solution.py:535
  43.0 1.3 %copy.10 = f32[2,256]{1,0:T(2,128)} copy(f32[2,256]{1,0:T(2,128)} %shard_map.82) | data formatting | bytes 4096

commit v8 on v7

--- a/solution.py
+++ b/solution.py
@@ -277,19 +277,18 @@
             total = summed(0)
         length = tlen[z] - x * BLOCK
         twice, outputs, turned = finished(total, length)
-        products = jnp.dot(
-            turned, jnp.concatenate([outputs, twice], axis=1), preferred_element_type=F32
-        )
+        outs = jnp.dot(turned, outputs, preferred_element_type=F32)
         ins = lax.dot_general(
             twice, twice, (((0,), (0,)), ((), ())), preferred_element_type=F32
         )
         live = jnp.minimum(jnp.maximum(length, 0), BLOCK).astype(F32)
-        part[0:4] = fold(products[:, :BLOCK]).reshape(4, 16, BLOCK)
+        part[0:4] = fold(outs).reshape(4, 16, BLOCK)
         part[4:8] = jnp.where(left, ins[:HALF], live).reshape(4, 16, BLOCK)
         for m in range(7, 0, -1):
             moment1(m).start()
         unless(leads)(lambda: moment1(0).start())
-        part[40:44] = fold(products[:, BLOCK:]).reshape(4, 16, BLOCK)
+        sketch = jnp.dot(turned, twice, preferred_element_type=F32)
+        part[40:44] = fold(sketch).reshape(4, 16, BLOCK)
         for m in range(1, 4):
             sketch1(m).start()
 
@@ -491,7 +490,7 @@
         def _():
             do("phase2_0", phase2, 0)
 
-        @pl.when(four == 4)
+        @pl.when(four == 5)
         def _():
             phase1(2)
 

time: 44.4 us -> 44.3 us (level)
  no operation moved by 1% of the time
where the time goes in v8:
time: 44.3 us; the launch traced here: 44.1 us
  Pallas kernels  42.9 us (97%)
  local copies, waits for them, and re-layouts  1.26 us (3%)
    pallas_call x1, Pallas kernels, on_device(): pl.pallas_call(kernel, out_shape=jax.ShapeDtypeStruct((tin.shape[0], DP *...  42.9 us
    unnamed x1, local copies, waits for them, and re-layouts  1.26 us

profile of v8, /device:TPU:1, one launch (start us, length us, event | category | flops | bytes accessed | tf_op | source)
XLA Modules:
  0.0 44.1 jit_solution(12165056870150685383)
XLA Ops:
  0.0 42.9 %shard_map.82 = f32[2,256]{1,0:T(2,128)} custom-call(s32[2]{0:T(128)} %tlen_hbm.1, s32[16]{0:T(128)} %qlen_hbm.1, bf16[2,512,512]{2,1,0:T(8,128)(2,1)} %tin.1, bf16[2,2,512,1792]{3,2,1,0:T(8,128)(2,1)} %tgr.1, bf16[16,128,512]{2,1,0:T(8,128)(2,1)} %qin.1, bf16[16,2,128,1792]{3,2,1,0:T(8,128)(2,1)} %qgr.1, bf16[64,512]{1,0:T(8,128)(2,1)} %bitcast.3, ...), custom_call_target="tpu_custom_call" | custom-call | tf_op jit(solution)/shard_map/pallas_call | solution.py:534
  42.9 1.3 %copy.10 = f32[2,256]{1,0:T(2,128)} copy(f32[2,256]{1,0:T(2,128)} %shard_map.82) | data formatting | bytes 4096

commit v9 on v8

--- a/solution.py
+++ b/solution.py
@@ -369,7 +369,7 @@
         weight, start = chebyshev()
 
         def double(i, carry):
-            pl.when(i == 5)(swap_sketches)
+            pl.when(i == 4)(swap_sketches)
             value, state = carry
             following = 2.0 * value * value - 1.0
             g = 2.0 * value * value / following
@@ -500,8 +500,8 @@
     do("moments_over_dp", moments_over_dp)
     do("phase2_2", phase2, 2)
     do("share_1", share_sketch, 1)
+    do("sketches_across", sketches_across)
     do("moments_back", moments_back)
-    do("sketches_across", sketches_across)
     do("share_2", share_sketch, 2)
     inv_out, inv_in = do("inverses", inverses)
     weights = do("solve", solve, inv_out, inv_in)

time: 44.3 us -> 44.4 us (level)
  no operation moved by 1% of the time
where the time goes in v9:
time: 44.4 us; the launch traced here: 44.3 us
  Pallas kernels  43 us (97%)
  local copies, waits for them, and re-layouts  1.26 us (3%)
    pallas_call x1, Pallas kernels, on_device(): pl.pallas_call(kernel, out_shape=jax.ShapeDtypeStruct((tin.shape[0], DP *...  43 us
    unnamed x1, local copies, waits for them, and re-layouts  1.26 us

profile of v9, /device:TPU:1, one launch (start us, length us, event | category | flops | bytes accessed | tf_op | source)
XLA Modules:
  0.0 44.3 jit_solution(4845238643432491010)
XLA Ops:
  0.0 43.0 %shard_map.82 = f32[2,256]{1,0:T(2,128)} custom-call(s32[2]{0:T(128)} %tlen_hbm.1, s32[16]{0:T(128)} %qlen_hbm.1, bf16[2,512,512]{2,1,0:T(8,128)(2,1)} %tin.1, bf16[2,2,512,1792]{3,2,1,0:T(8,128)(2,1)} %tgr.1, bf16[16,128,512]{2,1,0:T(8,128)(2,1)} %qin.1, bf16[16,2,128,1792]{3,2,1,0:T(8,128)(2,1)} %qgr.1, bf16[64,512]{1,0:T(8,128)(2,1)} %bitcast.3, ...), custom_call_target="tpu_custom_call" | custom-call | tf_op jit(solution)/shard_map/pallas_call | solution.py:534
  43.0 1.3 %copy.10 = f32[2,256]{1,0:T(2,128)} copy(f32[2,256]{1,0:T(2,128)} %shard_map.82) | data formatting | bytes 4096
